TPU v7x, 256 devices: a whole 4x4x8 slice. The times are simulated.
256 devices in a mesh: gx: 8 (over x, core), gy: 8 (over z), gz: 4 (over y).
Axes of the slice: x: 4, y: 4, z: 8, core: 2. Of those that a mesh axis runs over, the one named last changes fastest.
Arguments:
- positions: float32 [3, 16, 16, 16, 128], P(None, 'gx', 'gy', 'gz'), may hold values from 0 to 11
- velocities: float32 [3, 16, 16, 16, 128], P(None, 'gx', 'gy', 'gz'), may hold values from -0.6 to 0.6
- counts: int32 [16, 16, 16], P('gx', 'gy', 'gz'), may hold values from 96 to 128
Outputs:
- new_velocity: float32 [3, 16, 16, 16, 128], P(None, 'gx', 'gy', 'gz')
- moved: float32 [3, 16, 16, 16, 128], P(None, 'gx', 'gy', 'gz')
All inputs are finite; a program needn't handle non-finite values.
Results may differ from a plain program's by a relative error of at most 0.0003.
Values sent between devices are 32-bit elements; how exact they have to be, the bound alone decides.
A program may use at most 64 MiB of HBM per device.

v0:
```python
import jax
import jax.numpy as jnp
from jax import lax
from jax.sharding import PartitionSpec as P

CELL_EDGE = 11.0
CUT_SQ = 25.0
WIDTH_DENSITY = 4.0
WIDTH_PAIR = 2.0
SCALE_DENSITY = 0.4
SCALE_PAIR = 0.3
DENSITY_REF = 1.0
TIME_STEP = 0.5
BOX_PAIRS = (
    ((0, 0, 0), (1, 0, 0)),
    ((0, 0, 0), (0, 1, 0)),
    ((0, 0, 0), (0, 0, 1)),
    ((0, 0, 0), (1, 1, 0)),
    ((0, 0, 0), (1, 0, 1)),
    ((0, 0, 0), (0, 1, 1)),
    ((0, 0, 0), (1, 1, 1)),
    ((0, 1, 0), (1, 0, 0)),
    ((0, 0, 1), (1, 0, 0)),
    ((0, 0, 1), (0, 1, 0)),
    ((0, 1, 0), (1, 0, 1)),
    ((0, 0, 1), (1, 1, 0)),
    ((1, 0, 0), (0, 1, 1)),
)


def from_behind(value, axis, steps):
    count = lax.axis_size(axis)
    pairs = [(source, (source + steps) % count) for source in range(count)]
    return lax.ppermute(value, axis, pairs)


def smooth_parts(radius_sq):
    inside = radius_sq < CUT_SQ
    remain = 1.0 - radius_sq / CUT_SQ
    smooth = jnp.where(inside, remain * remain, 0.0)
    smooth_slope = jnp.where(inside, -2.0 * remain / CUT_SQ, 0.0)
    return (smooth, smooth_slope)


def separation_of(slab_a, slab_b, offset):
    shift_vec = jnp.array(offset, jnp.float32) * CELL_EDGE
    return slab_b[:, :, None, :] - slab_a[:, :, :, None] + shift_vec[:, None, None, None]


def tile_weight(mask_a, mask_b, self_tile):
    weight = mask_a[:, :, None] * mask_b[:, None, :]
    if self_tile:
        weight = weight * (1.0 - jnp.eye(mask_a.shape[1], dtype=mask_a.dtype))
    return weight


def pair_density(slab_a, slab_b, mask_a, mask_b, offset, self_tile):
    separation = separation_of(slab_a, slab_b, offset)
    radius_sq = jnp.sum(separation * separation, axis=0)
    smooth, unused_slope = smooth_parts(radius_sq)
    pair_term = (
        tile_weight(mask_a, mask_b, self_tile)
        * SCALE_DENSITY
        * jnp.exp(-radius_sq / WIDTH_DENSITY)
        * smooth
    )
    return (jnp.sum(pair_term, axis=2), jnp.sum(pair_term, axis=1))


def pair_force(slab_a, slab_b, mask_a, mask_b, grad_a, grad_b, offset, self_tile):
    separation = separation_of(slab_a, slab_b, offset)
    radius_sq = jnp.sum(separation * separation, axis=0)
    smooth, smooth_slope = smooth_parts(radius_sq)
    density_fall = SCALE_DENSITY * jnp.exp(-radius_sq / WIDTH_DENSITY)
    density_slope = density_fall * (smooth_slope - smooth / WIDTH_DENSITY)
    pair_fall = SCALE_PAIR * jnp.exp(-radius_sq / WIDTH_PAIR)
    pair_slope = pair_fall * (smooth_slope - smooth / WIDTH_PAIR)
    factor = (
        tile_weight(mask_a, mask_b, self_tile)
        * 2.0
        * (pair_slope + (grad_a[:, :, None] + grad_b[:, None, :]) * density_slope)
    )
    pushed = factor[None] * separation
    return (jnp.sum(pushed, axis=3), -jnp.sum(pushed, axis=2))


def pick_block(most):
    for candidate in range(most, 0, -1):
        return candidate
    return 1


def take_cells(field, first_cell, block_size, axis_index):
    return lax.dynamic_slice_in_dim(field, first_cell, block_size, axis_index)


def density_sweep(slab_a, slab_b, mask_a, mask_b, offset, self_tile, most):
    cell_count, slot_count = mask_a.shape
    block_size = pick_block(most)
    empty_sums = jnp.zeros((cell_count, slot_count), jnp.float32)

    def density_visit_block(block_index, running):
        row_sums, col_sums = running
        first_cell = (block_index * block_size).astype(jnp.int32)
        row_block, col_block = pair_density(
            take_cells(slab_a, first_cell, block_size, 1),
            take_cells(slab_b, first_cell, block_size, 1),
            take_cells(mask_a, first_cell, block_size, 0),
            take_cells(mask_b, first_cell, block_size, 0),
            offset,
            self_tile,
        )
        row_sums = lax.dynamic_update_slice_in_dim(row_sums, row_block, first_cell, 0)
        col_sums = lax.dynamic_update_slice_in_dim(col_sums, col_block, first_cell, 0)
        return (row_sums, col_sums)

    return lax.fori_loop(0, cell_count // block_size, density_visit_block, (empty_sums, empty_sums))


def force_sweep(slab_a, slab_b, mask_a, mask_b, grad_a, grad_b, offset, self_tile, most):
    cell_count, slot_count = mask_a.shape
    block_size = pick_block(most)
    empty_push = jnp.zeros((3, cell_count, slot_count), jnp.float32)

    def force_visit_block(block_index, running):
        push_a, push_b = running
        first_cell = (block_index * block_size).astype(jnp.int32)
        block_a, block_b = pair_force(
            take_cells(slab_a, first_cell, block_size, 1),
            take_cells(slab_b, first_cell, block_size, 1),
            take_cells(mask_a, first_cell, block_size, 0),
            take_cells(mask_b, first_cell, block_size, 0),
            take_cells(grad_a, first_cell, block_size, 0),
            take_cells(grad_b, first_cell, block_size, 0),
            offset,
            self_tile,
        )
        push_a = lax.dynamic_update_slice_in_dim(push_a, block_a, first_cell, 1)
        push_b = lax.dynamic_update_slice_in_dim(push_b, block_b, first_cell, 1)
        return (push_a, push_b)

    return lax.fori_loop(0, cell_count // block_size, force_visit_block, (empty_push, empty_push))


def cut_cells(field, corner, extent):
    picked = field[
        :,
        corner[0] : corner[0] + extent[0],
        corner[1] : corner[1] + extent[1],
        corner[2] : corner[2] + extent[2],
    ]
    return picked.reshape(field.shape[0], extent[0] * extent[1] * extent[2], field.shape[4])


def place_cells(field, corner, extent, block_sums):
    shaped = block_sums.reshape(field.shape[0], extent[0], extent[1], extent[2], field.shape[4])
    return field.at[
        :,
        corner[0] : corner[0] + extent[0],
        corner[1] : corner[1] + extent[1],
        corner[2] : corner[2] + extent[2],
    ].add(shaped)


def import_forward(field):
    front = from_behind(field[:, 0:1], "gx", -1)
    field = jnp.concatenate([field, front], axis=1)
    front = from_behind(field[:, :, 0:1], "gy", -1)
    field = jnp.concatenate([field, front], axis=2)
    front = from_behind(field[:, :, :, 0:1], "gz", -1)
    return jnp.concatenate([field, front], axis=3)


def fold_back(field):
    inner_z = field.shape[3] - 1
    border = from_behind(field[:, :, :, inner_z:], "gz", 1)
    field = field[:, :, :, :inner_z].at[:, :, :, 0:1].add(border)
    inner_y = field.shape[2] - 1
    border = from_behind(field[:, :, inner_y:], "gy", 1)
    field = field[:, :, :inner_y].at[:, :, 0:1].add(border)
    inner_x = field.shape[1] - 1
    border = from_behind(field[:, inner_x:], "gx", 1)
    return field[:, :inner_x].at[:, 0:1].add(border)


def total_forces(positions, live):
    size_x, size_y, size_z, slot_count = live.shape
    extent = (size_x, size_y, size_z)
    cell_count = size_x * size_y * size_z
    packed = jnp.concatenate([positions, live[None]], axis=0)
    own_pos = positions.reshape(3, cell_count, slot_count)
    own_live = live.reshape(cell_count, slot_count)
    extended = import_forward(packed)
    density = jnp.zeros((1, size_x + 1, size_y + 1, size_z + 1, slot_count), jnp.float32)
    row_block, unused_cols = density_sweep(own_pos, own_pos, own_live, own_live, (0, 0, 0), True, 8)
    density = place_cells(density, (0, 0, 0), extent, row_block[None])
    for corner_a, corner_b in BOX_PAIRS:
        offset = (corner_b[0] - corner_a[0], corner_b[1] - corner_a[1], corner_b[2] - corner_a[2])
        piece_a = cut_cells(extended, corner_a, extent)
        piece_b = cut_cells(extended, corner_b, extent)
        row_block, col_block = density_sweep(
            piece_a[:3], piece_b[:3], piece_a[3], piece_b[3], offset, False, 8
        )
        density = place_cells(density, corner_a, extent, row_block[None])
        density = place_cells(density, corner_b, extent, col_block[None])
    density = fold_back(density)[0].reshape(cell_count, slot_count)
    embed_grad = own_live * 2.0 * (density - DENSITY_REF)
    grad_ext = import_forward(embed_grad.reshape(1, size_x, size_y, size_z, slot_count))
    forces = jnp.zeros((3, size_x + 1, size_y + 1, size_z + 1, slot_count), jnp.float32)
    push_a, unused_push = force_sweep(
        own_pos, own_pos, own_live, own_live, embed_grad, embed_grad, (0, 0, 0), True, 8
    )
    forces = place_cells(forces, (0, 0, 0), extent, push_a)
    for corner_a, corner_b in BOX_PAIRS:
        offset = (corner_b[0] - corner_a[0], corner_b[1] - corner_a[1], corner_b[2] - corner_a[2])
        piece_a = cut_cells(extended, corner_a, extent)
        piece_b = cut_cells(extended, corner_b, extent)
        grad_a = cut_cells(grad_ext, corner_a, extent)[0]
        grad_b = cut_cells(grad_ext, corner_b, extent)[0]
        push_a, push_b = force_sweep(
            piece_a[:3], piece_b[:3], piece_a[3], piece_b[3], grad_a, grad_b, offset, False, 8
        )
        forces = place_cells(forces, corner_a, extent, push_a)
        forces = place_cells(forces, corner_b, extent, push_b)
    return fold_back(forces)


def live_slots(counts, slot_count):
    slot_index = lax.broadcasted_iota(jnp.int32, counts.shape + (slot_count,), 3)
    return (slot_index < counts[..., None]).astype(jnp.float32)


def body(positions, velocities, counts):
    live = live_slots(counts, positions.shape[4])
    running_position = positions
    running_velocity = velocities
    forces = total_forces(running_position, live)
    running_velocity = running_velocity + TIME_STEP * forces
    running_position = running_position + TIME_STEP * running_velocity
    return (running_velocity * live[None], (running_position - positions) * live[None])


def solution(mesh):
    return jax.shard_map(
        body,
        mesh=mesh,
        in_specs=(
            P(None, "gx", "gy", "gz", None),
            P(None, "gx", "gy", "gz", None),
            P("gx", "gy", "gz"),
        ),
        out_specs=(P(None, "gx", "gy", "gz", None), P(None, "gx", "gy", "gz", None)),
        check_vma=False,
    )
```

profile of v0, /device:TPU:0, one launch (start us, length us, event | category | flops | bytes accessed | tf_op | source)
XLA Modules:
  0.0 145.6 jit_solution(9175480394886173465)
XLA Ops:
  4.8 5.9 %collective-permute-start.1 = (f32[4,3,1,4,128]{4,3,2,1,0:T(4,128)S(1)}, f32[4,3,1,4,128]{4,3,2,1,0:T(4,128)S(1)}, u32[]{:S(2)}, u32[]{:S(2)}) collective-permute-start(f32[4,3,1,4,128]{4,3,2,1,0:T(4,128)S(1)} %slice.2796), channel_id=1, source_target_pairs={{0,28},{4,0},{8,4},{12,8},{16,12},{20,16},{24,20},{28,24},{1,29},{... | collective-permute-start | bytes 73736 | tf_op jit(solution)/shard_map/ppermute | solution.py:34
  10.7 3.3 %while.532 = (s32[]{:T(128)}, f32[16,128]{1,0:T(8,128)S(1)}, f32[16,128]{1,0:T(8,128)S(1)}, f32[3,16,128]{2,1,0:T(8,128)}, s32[]{:T(128)}, /*index=5*/s32[]{:T(128)}, s32[]{:T(128)}, s32[]{:T(128)}) while((s32[]{:T(128)}, f32[16,128]{1,0:T(8,128)S(1)}, f32[16,128]{1,0:T(8,128)S(1)}, f32[3,16,128]{2,1,0:T(8,128)}, s32[]{:T(128)}, ...), condition=%wide.region_3.4_spmd.clone, body=%wide.region_0.3_spmd.sunk.clone.sunk | while | flops 2800646 | bytes 1241239 | solution.py:117
  14.9 3.1 %collective-permute-start.2 = (f32[4,3,3,1,128]{4,3,2,1,0:T(1,128)S(1)}, f32[4,3,3,1,128]{4,3,2,1,0:T(1,128)S(1)}, u32[]{:S(2)}, u32[]{:S(2)}) collective-permute-start(f32[4,3,3,1,128]{4,3,2,1,0:T(1,128)S(1)} %slice.2800), channel_id=1, source_target_pairs={{0,3},{1,0},{2,1},{3,2},{4,7},{5,4},{6,5},{7,6},{8,11},{9,8},{10,9... | collective-permute-start | bytes 55304 | tf_op jit(solution)/shard_map/ppermute | solution.py:34
  19.5 2.5 %while.533 = (s32[]{:T(128)}, f32[16,128]{1,0:T(8,128)S(1)}, f32[16,128]{1,0:T(8,128)S(1)}, f32[16,128]{1,0:T(8,128)S(1)}, f32[16,128]{1,0:T(8,128)S(1)}, /*inde...) while((s32[]{:T(128)}, f32[16,128]{1,0:T(8,128)S(1)}, ...), condition=%wide.region_8.0_spmd.clone, body=%wide.region_4.8_spmd.sunk.clone.sunk | while | flops 3143686 | bytes 1171659 | solution.py:117
  22.1 2.0 %while.534 = (s32[]{:T(128)}, f32[16,128]{1,0:T(8,128)S(1)}, f32[16,128]{1,0:T(8,128)S(1)}, f32[16,128]{1,0:T(8,128)S(1)}, f32[16,128]{1,0:T(8,128)S(1)}, /*inde...) while((s32[]{:T(128)}, f32[16,128]{1,0:T(8,128)S(1)}, ...), condition=%wide.region_13.0_spmd.clone, body=%wide.region_9.13_spmd.sunk.clone.sunk | while | flops 3143686 | bytes 1171659 | solution.py:117
  24.2 2.0 %while.535 = (s32[]{:T(128)}, f32[16,128]{1,0:T(8,128)S(1)}, f32[16,128]{1,0:T(8,128)S(1)}, f32[16,128]{1,0:T(8,128)S(1)}, f32[16,128]{1,0:T(8,128)S(1)}, /*inde...) while((s32[]{:T(128)}, f32[16,128]{1,0:T(8,128)S(1)}, ...), condition=%wide.region_18.19_spmd.clone, body=%wide.region_14.18_spmd.sunk.clone.sunk | while | flops 3143686 | bytes 1171659 | solution.py:117
  26.4 2.0 %while.536 = (s32[]{:T(128)}, f32[16,128]{1,0:T(8,128)S(1)}, f32[16,128]{1,0:T(8,128)S(1)}, f32[16,128]{1,0:T(8,128)S(1)}, f32[16,128]{1,0:T(8,128)S(1)}, /*inde...) while((s32[]{:T(128)}, f32[16,128]{1,0:T(8,128)S(1)}, ...), condition=%wide.region_23.24_spmd.clone, body=%wide.region_19.23_spmd.sunk.clone.sunk | while | flops 3143686 | bytes 1171659 | solution.py:117
  35.1 2.0 %while.540 = (s32[]{:T(128)}, f32[16,128]{1,0:T(8,128)S(1)}, f32[16,128]{1,0:T(8,128)S(1)}, f32[16,128]{1,0:T(8,128)S(1)}, f32[16,128]{1,0:T(8,128)S(1)}, /*inde...) while((s32[]{:T(128)}, f32[16,128]{1,0:T(8,128)S(1)}, ...), condition=%wide.region_43.0_spmd.clone, body=%wide.region_39.43_spmd.sunk.clone.sunk | while | flops 3143686 | bytes 1171659 | solution.py:117
  43.8 2.0 %while.544 = (s32[]{:T(128)}, f32[16,128]{1,0:T(8,128)S(1)}, f32[16,128]{1,0:T(8,128)S(1)}, f32[16,128]{1,0:T(8,128)S(1)}, f32[16,128]{1,0:T(8,128)S(1)}, /*inde...) while((s32[]{:T(128)}, f32[16,128]{1,0:T(8,128)S(1)}, ...), condition=%wide.region_63.0_spmd.clone, body=%wide.region_59.63_spmd.sunk.clone.sunk | while | flops 3143686 | bytes 1171659 | solution.py:117
  46.0 2.2 %while.545 = (s32[]{:T(128)}, f32[16,128]{1,0:T(8,128)S(1)}, f32[16,128]{1,0:T(8,128)S(1)}, f32[16,128]{1,0:T(8,128)S(1)}, f32[16,128]{1,0:T(8,128)S(1)}, /*inde...) while((s32[]{:T(128)}, f32[16,128]{1,0:T(8,128)S(1)}, ...), condition=%wide.region_68.69_spmd.clone, body=%wide.region_64.68_spmd.sunk.clone.sunk | while | flops 3143686 | bytes 1171659 | solution.py:117
  49.3 4.2 %collective-permute-done.3 = f32[1,3,3,1,128]{4,3,2,1,0:T(1,128)S(1)} collective-permute-done((f32[1,3,3,1,128]{4,3,2,1,0:T(1,128)S(1)}, f32[1,3,3,1,128]{4,3,2,1,0:T(1,128)S(1)}, u32[]{:S(2)}, u32[]{:S(2)}) %collective-permute-start.3) | collective-permute-done | bytes 4640 | tf_op jit(solution)/shard_map/ppermute | solution.py:34
  53.7 4.8 %collective-permute-done.4 = f32[1,3,1,4,128]{4,3,2,1,0:T(4,128)S(1)} collective-permute-done((f32[1,3,1,4,128]{4,3,2,1,0:T(4,128)S(1)}, f32[1,3,1,4,128]{4,3,2,1,0:T(4,128)S(1)}, u32[]{:S(2)}, u32[]{:S(2)}) %collective-permute-start.4) | collective-permute-done | bytes 6176 | tf_op jit(solution)/shard_map/ppermute | solution.py:34
  58.5 4.2 %collective-permute-done.5 = f32[1,1,2,4,128]{4,3,2,1,0:T(4,128)S(1)} collective-permute-done((f32[1,1,2,4,128]{4,3,2,1,0:T(4,128)S(1)}, f32[1,1,2,4,128]{4,3,2,1,0:T(4,128)S(1)}, u32[]{:S(2)}, u32[]{:S(2)}) %collective-permute-start.5) | collective-permute-done | bytes 4128 | tf_op jit(solution)/shard_map/ppermute | solution.py:34
  62.9 4.0 %while.546 = (s32[]{:T(128)}, f32[3,16,128]{2,1,0:T(8,128)S(1)}, f32[16,128]{1,0:T(8,128)S(1)}, f32[3,16,128]{2,1,0:T(8,128)S(1)}, f32[16,128]{1,0:T(8,128)S(1)}...) while((s32[]{:T(128)}, f32[3,16,128]{2,1,0:T(8,128)S(1)}, f32[16,128]{1,0:T(8,128)S(1)}, ...), condition=%wide.region_72.73_spmd.clone, body=%wide.region_69.72_spmd.sunk.clone.sunk | while | flops 5551110 | bytes 2338975 | solution.py:142
  67.0 4.1 %while.547 = (s32[]{:T(128)}, f32[3,16,128]{2,1,0:T(8,128)S(1)}, f32[3,16,128]{2,1,0:T(8,128)S(1)}, f32[16,128]{1,0:T(8,128)S(1)}, f32[16,128]{1,0:T(8,128)S(1)}...) while((s32[]{:T(128)}, f32[3,16,128]{2,1,0:T(8,128)S(1)}, ...), condition=%wide.region_77.0_spmd.clone, body=%wide.region_73.77_spmd.sunk.clone.sunk | while | flops 6550534 | bytes 2318575 | solution.py:142
  71.7 3.2 %collective-permute-done.7 = f32[1,3,1,4,128]{4,3,2,1,0:T(4,128)S(1)} collective-permute-done((f32[1,3,1,4,128]{4,3,2,1,0:T(4,128)S(1)}, f32[1,3,1,4,128]{4,3,2,1,0:T(4,128)S(1)}, u32[]{:S(2)}, u32[]{:S(2)}) %collective-permute-start.7) | collective-permute-done | bytes 6176 | tf_op jit(solution)/shard_map/ppermute | solution.py:34
  74.9 4.1 %while.548 = (s32[]{:T(128)}, f32[3,16,128]{2,1,0:T(8,128)S(1)}, f32[3,16,128]{2,1,0:T(8,128)S(1)}, f32[16,128]{1,0:T(8,128)S(1)}, f32[16,128]{1,0:T(8,128)S(1)}...) while((s32[]{:T(128)}, f32[3,16,128]{2,1,0:T(8,128)S(1)}, ...), condition=%wide.region_82.83_spmd.clone, body=%wide.region_78.82_spmd.sunk.clone.sunk | while | flops 6550534 | bytes 2318575 | solution.py:142
  79.1 2.1 %collective-permute-start.8 = (f32[1,3,3,1,128]{4,3,2,1,0:T(1,128)S(1)}, f32[1,3,3,1,128]{4,3,2,1,0:T(1,128)S(1)}, u32[]{:S(2)}, u32[]{:S(2)}) collective-permute-start(f32[1,3,3,1,128]{4,3,2,1,0:T(1,128)S(1)} %pad_maximum_fusion.22), channel_id=1, source_target_pairs={{0,3},{1,0},{2,1},{3,2},{4,7},{5,4},{6,5},{7,6},{8,11},{9,8},{10,9... | collective-permute-start | bytes 13832 | tf_op jit(solution)/shard_map/ppermute | solution.py:34
  81.2 4.3 %while.554 = (s32[]{:T(128)}, f32[3,16,128]{2,1,0:T(8,128)S(1)}, f32[3,16,128]{2,1,0:T(8,128)S(1)}, f32[16,128]{1,0:T(8,128)S(1)}, f32[16,128]{1,0:T(8,128)S(1)}...) while((s32[]{:T(128)}, f32[3,16,128]{2,1,0:T(8,128)S(1)}, ...), condition=%wide.region_112.0_spmd.clone, body=%wide.region_108.112_spmd.sunk.clone.sunk | while | flops 6550534 | bytes 2318575 | solution.py:142
  85.7 4.1 %while.549 = (s32[]{:T(128)}, f32[3,16,128]{2,1,0:T(8,128)S(1)}, f32[3,16,128]{2,1,0:T(8,128)S(1)}, f32[16,128]{1,0:T(8,128)S(1)}, f32[16,128]{1,0:T(8,128)S(1)}...) while((s32[]{:T(128)}, f32[3,16,128]{2,1,0:T(8,128)S(1)}, ...), condition=%wide.region_87.88_spmd.clone, body=%wide.region_83.87_spmd.sunk.clone.sunk | while | flops 6550534 | bytes 2318575 | solution.py:142
  90.0 4.1 %while.550 = (s32[]{:T(128)}, f32[3,16,128]{2,1,0:T(8,128)S(1)}, f32[3,16,128]{2,1,0:T(8,128)S(1)}, f32[16,128]{1,0:T(8,128)S(1)}, f32[16,128]{1,0:T(8,128)S(1)}...) while((s32[]{:T(128)}, f32[3,16,128]{2,1,0:T(8,128)S(1)}, ...), condition=%wide.region_92.0_spmd.clone, body=%wide.region_88.92_spmd.sunk.clone.sunk | while | flops 6550534 | bytes 2318575 | solution.py:142
  94.2 4.1 %while.551 = (s32[]{:T(128)}, f32[3,16,128]{2,1,0:T(8,128)S(1)}, f32[3,16,128]{2,1,0:T(8,128)S(1)}, f32[16,128]{1,0:T(8,128)S(1)}, f32[16,128]{1,0:T(8,128)S(1)}...) while((s32[]{:T(128)}, f32[3,16,128]{2,1,0:T(8,128)S(1)}, ...), condition=%wide.region_97.98_spmd.clone, body=%wide.region_93.97_spmd.sunk.clone.sunk | while | flops 6550534 | bytes 2318575 | solution.py:142
  98.6 4.1 %while.552 = (s32[]{:T(128)}, f32[3,16,128]{2,1,0:T(8,128)S(1)}, f32[3,16,128]{2,1,0:T(8,128)S(1)}, f32[16,128]{1,0:T(8,128)S(1)}, f32[16,128]{1,0:T(8,128)S(1)}...) while((s32[]{:T(128)}, f32[3,16,128]{2,1,0:T(8,128)S(1)}, ...), condition=%wide.region_102.103_spmd.clone, body=%wide.region_98.102_spmd.sunk.clone.sunk | while | flops 6550534 | bytes 2318575 | solution.py:142
  103.0 4.4 %while.553 = (s32[]{:T(128)}, f32[3,16,128]{2,1,0:T(8,128)S(1)}, f32[3,16,128]{2,1,0:T(8,128)S(1)}, f32[16,128]{1,0:T(8,128)S(1)}, f32[16,128]{1,0:T(8,128)S(1)}...) while((s32[]{:T(128)}, f32[3,16,128]{2,1,0:T(8,128)S(1)}, ...), condition=%wide.region_107.0_spmd.clone, body=%wide.region_103.107_spmd.sunk.clone.sunk | while | flops 6550534 | bytes 2318543 | solution.py:142
  107.6 4.1 %while.555 = (s32[]{:T(128)}, f32[3,16,128]{2,1,0:T(8,128)S(1)}, f32[3,16,128]{2,1,0:T(8,128)S(1)}, f32[16,128]{1,0:T(8,128)S(1)}, f32[16,128]{1,0:T(8,128)S(1)}...) while((s32[]{:T(128)}, f32[3,16,128]{2,1,0:T(8,128)S(1)}, ...), condition=%wide.region_117.118_spmd.clone, body=%wide.region_113.117_spmd.sunk.clone.sunk | while | flops 6550534 | bytes 2318575 | solution.py:142
  112.0 4.1 %while.556 = (s32[]{:T(128)}, f32[3,16,128]{2,1,0:T(8,128)S(1)}, f32[3,16,128]{2,1,0:T(8,128)S(1)}, f32[16,128]{1,0:T(8,128)S(1)}, f32[16,128]{1,0:T(8,128)S(1)}...) while((s32[]{:T(128)}, f32[3,16,128]{2,1,0:T(8,128)S(1)}, ...), condition=%wide.region_122.123_spmd.clone, body=%wide.region_118.122_spmd.sunk.clone.sunk | while | flops 6550534 | bytes 2318575 | solution.py:142
  116.4 4.1 %while.557 = (s32[]{:T(128)}, f32[3,16,128]{2,1,0:T(8,128)S(1)}, f32[3,16,128]{2,1,0:T(8,128)S(1)}, f32[16,128]{1,0:T(8,128)S(1)}, f32[16,128]{1,0:T(8,128)S(1)}...) while((s32[]{:T(128)}, f32[3,16,128]{2,1,0:T(8,128)S(1)}, ...), condition=%wide.region_127.0_spmd.clone, body=%wide.region_123.127_spmd.sunk.clone.sunk | while | flops 6550534 | bytes 2318575 | solution.py:142
  120.8 4.1 %while.558 = (s32[]{:T(128)}, f32[3,16,128]{2,1,0:T(8,128)S(1)}, f32[3,16,128]{2,1,0:T(8,128)S(1)}, f32[16,128]{1,0:T(8,128)S(1)}, f32[16,128]{1,0:T(8,128)S(1)}...) while((s32[]{:T(128)}, f32[3,16,128]{2,1,0:T(8,128)S(1)}, ...), condition=%wide.region_132.133_spmd.clone, body=%wide.region_128.132_spmd.sunk.clone.sunk | while | flops 6550534 | bytes 2318575 | solution.py:142
  125.2 4.4 %while.559 = (s32[]{:T(128)}, f32[3,16,128]{2,1,0:T(8,128)S(1)}, f32[3,16,128]{2,1,0:T(8,128)S(1)}, f32[16,128]{1,0:T(8,128)S(1)}, f32[16,128]{1,0:T(8,128)S(1)}...) while((s32[]{:T(128)}, f32[3,16,128]{2,1,0:T(8,128)S(1)}, ...), condition=%wide.region_137.138_spmd.clone, body=%wide.region_133.137_spmd.sunk.clone.sunk | while | flops 6550534 | bytes 2318575 | solution.py:142
  130.0 4.9 %collective-permute-done.9 = f32[3,3,3,1,128]{4,3,2,1,0:T(1,128)S(1)} collective-permute-done((f32[3,3,3,1,128]{4,3,2,1,0:T(1,128)S(1)}, f32[3,3,3,1,128]{4,3,2,1,0:T(1,128)S(1)}, u32[]{:S(2)}, u32[]{:S(2)}) %collective-permute-start.9) | collective-permute-done | bytes 13856 | tf_op jit(solution)/shard_map/ppermute | solution.py:34
  135.1 4.9 %collective-permute-done.10 = f32[3,3,1,4,128]{4,3,2,1,0:T(4,128)S(1)} collective-permute-done((f32[3,3,1,4,128]{4,3,2,1,0:T(4,128)S(1)}, f32[3,3,1,4,128]{4,3,2,1,0:T(4,128)S(1)}, u32[]{:S(2)}, u32[]{:S(2)}) %collective-permute-start.10) | collective-permute-done | bytes 18464 | tf_op jit(solution)/shard_map/ppermute | solution.py:34
  140.2 4.2 %collective-permute-done.11 = f32[3,1,2,4,128]{4,3,2,1,0:T(4,128)S(1)} collective-permute-done((f32[3,1,2,4,128]{4,3,2,1,0:T(4,128)S(1)}, f32[3,1,2,4,128]{4,3,2,1,0:T(4,128)S(1)}, u32[]{:S(2)}, u32[]{:S(2)}) %collective-permute-start.11) | collective-permute-done | bytes 12320 | tf_op jit(solution)/shard_map/ppermute | solution.py:34
  (692 shorter events, 107.2 us)
Async XLA Ops:
  2.1 1.9 %collective-permute-start = (f32[4,1,2,4,128]{4,3,2,1,0:T(4,128)S(1)}, f32[4,1,2,4,128]{4,3,2,1,0:T(4,128)S(1)}, u32[]{:S(2)}, u32[]{:S(2)}) collective-permute-start(f32[4,1,2,4,128]{4,3,2,1,0:T(4,128)S(1)} %pad_maximum_fusion.6), channel_id=1, source_target_pairs={{0,224},{32,0},{64,32},{96,64},{128,96},{160,128},{192,160},{224,1... | collective-permute-start | bytes 49160 | tf_op jit(solution)/shard_map/ppermute | solution.py:34
  4.8 9.3 %collective-permute-start.1 = (f32[4,3,1,4,128]{4,3,2,1,0:T(4,128)S(1)}, f32[4,3,1,4,128]{4,3,2,1,0:T(4,128)S(1)}, u32[]{:S(2)}, u32[]{:S(2)}) collective-permute-start(f32[4,3,1,4,128]{4,3,2,1,0:T(4,128)S(1)} %slice.2796), channel_id=1, source_target_pairs={{0,28},{4,0},{8,4},{12,8},{16,12},{20,16},{24,20},{28,24},{1,29},{... | collective-permute-start | bytes 73736 | tf_op jit(solution)/shard_map/ppermute | solution.py:34
  14.0 5.5 %copy-start = (f32[3,16,128]{2,1,0:T(8,128)S(1)}, f32[3,16,128]{2,1,0:T(8,128)}, u32[]{:S(2)}) copy-start(f32[3,16,128]{2,1,0:T(8,128)} %get-tuple-element.9901) | copy-start | bytes 73732
  14.0 5.5 %copy-start.12 = (f32[3]{0:T(128)S(1)}, f32[3]{0:T(128)}, u32[]{:S(2)}) copy-start(f32[3]{0:T(128)} %constant.4679) | copy-start | bytes 40
  14.9 4.6 %collective-permute-start.2 = (f32[4,3,3,1,128]{4,3,2,1,0:T(1,128)S(1)}, f32[4,3,3,1,128]{4,3,2,1,0:T(1,128)S(1)}, u32[]{:S(2)}, u32[]{:S(2)}) collective-permute-start(f32[4,3,3,1,128]{4,3,2,1,0:T(1,128)S(1)} %slice.2800), channel_id=1, source_target_pairs={{0,3},{1,0},{2,1},{3,2},{4,7},{5,4},{6,5},{7,6},{8,11},{9,8},{10,9... | collective-permute-start | bytes 55304 | tf_op jit(solution)/shard_map/ppermute | solution.py:34
  19.5 2.5 %copy-start.11 = (f32[3]{0:T(128)S(1)}, f32[3]{0:T(128)}, u32[]{:S(2)}) copy-start(f32[3]{0:T(128)} %constant.4682) | copy-start | bytes 40
  22.1 2.1 %copy-start.9 = (f32[3]{0:T(128)S(1)}, f32[3]{0:T(128)}, u32[]{:S(2)}) copy-start(f32[3]{0:T(128)} %constant.4685) | copy-start | bytes 40
  24.2 2.3 %copy-start.8 = (f32[3]{0:T(128)S(1)}, f32[3]{0:T(128)}, u32[]{:S(2)}) copy-start(f32[3]{0:T(128)} %constant.4688) | copy-start | bytes 40
  26.4 2.0 %copy-start.7 = (f32[3]{0:T(128)S(1)}, f32[3]{0:T(128)}, u32[]{:S(2)}) copy-start(f32[3]{0:T(128)} %constant.4691) | copy-start | bytes 40
  28.5 2.3 %copy-start.6 = (f32[3]{0:T(128)S(1)}, f32[3]{0:T(128)}, u32[]{:S(2)}) copy-start(f32[3]{0:T(128)} %constant.4694) | copy-start | bytes 40
  32.9 2.2 %copy-start.10 = (f32[3]{0:T(128)S(1)}, f32[3]{0:T(128)}, u32[]{:S(2)}) copy-start(f32[3]{0:T(128)} %constant.4698) | copy-start | bytes 40
  35.1 2.0 %copy-start.5 = (f32[3]{0:T(128)S(1)}, f32[3]{0:T(128)}, u32[]{:S(2)}) copy-start(f32[3]{0:T(128)} %constant.4701) | copy-start | bytes 40
  37.1 2.2 %copy-start.4 = (f32[3]{0:T(128)S(1)}, f32[3]{0:T(128)}, u32[]{:S(2)}) copy-start(f32[3]{0:T(128)} %constant.4704) | copy-start | bytes 40
  39.3 2.2 %copy-start.3 = (f32[3]{0:T(128)S(1)}, f32[3]{0:T(128)}, u32[]{:S(2)}) copy-start(f32[3]{0:T(128)} %constant.4707) | copy-start | bytes 40
  41.6 2.2 %copy-start.2 = (f32[3]{0:T(128)S(1)}, f32[3]{0:T(128)}, u32[]{:S(2)}) copy-start(f32[3]{0:T(128)} %constant.4710) | copy-start | bytes 40
  43.8 2.2 %copy-start.1 = (f32[3]{0:T(128)S(1)}, f32[3]{0:T(128)}, u32[]{:S(2)}) copy-start(f32[3]{0:T(128)} %constant.4713) | copy-start | bytes 40
  46.0 16.8 %copy-start.13 = (s32[2,2,4]{2,1,0:T(2,128)S(1)}, s32[2,2,4]{2,1,0:T(2,128)}, u32[]{:S(2)}) copy-start(s32[2,2,4]{2,1,0:T(2,128)} %param.209) | copy-start | bytes 196
  48.3 5.2 %collective-permute-start.3 = (f32[1,3,3,1,128]{4,3,2,1,0:T(1,128)S(1)}, f32[1,3,3,1,128]{4,3,2,1,0:T(1,128)S(1)}, u32[]{:S(2)}, u32[]{:S(2)}) collective-permute-start(f32[1,3,3,1,128]{4,3,2,1,0:T(1,128)S(1)} %slice.2826), channel_id=1, source_target_pairs={{0,1},{1,2},{2,3},{3,0},{4,5},{5,6},{6,7},{7,4},{8,9},{9,10},{10,1... | collective-permute-start | bytes 13832 | tf_op jit(solution)/shard_map/ppermute | solution.py:34
  53.6 4.9 %collective-permute-start.4 = (f32[1,3,1,4,128]{4,3,2,1,0:T(4,128)S(1)}, f32[1,3,1,4,128]{4,3,2,1,0:T(4,128)S(1)}, u32[]{:S(2)}, u32[]{:S(2)}) collective-permute-start(f32[1,3,1,4,128]{4,3,2,1,0:T(4,128)S(1)} %slice.2829), channel_id=1, source_target_pairs={{0,4},{4,8},{8,12},{12,16},{16,20},{20,24},{24,28},{28,0},{1,5},{5... | collective-permute-start | bytes 18440 | tf_op jit(solution)/shard_map/ppermute | solution.py:34
  58.5 4.2 %collective-permute-start.5 = (f32[1,1,2,4,128]{4,3,2,1,0:T(4,128)S(1)}, f32[1,1,2,4,128]{4,3,2,1,0:T(4,128)S(1)}, u32[]{:S(2)}, u32[]{:S(2)}) collective-permute-start(f32[1,1,2,4,128]{4,3,2,1,0:T(4,128)S(1)} %slice.2832), channel_id=1, source_target_pairs={{0,32},{32,64},{64,96},{96,128},{128,160},{160,192},{192,224},{224... | collective-permute-start | bytes 12296 | tf_op jit(solution)/shard_map/ppermute | solution.py:34
  62.9 4.1 %collective-permute-start.6 = (f32[1,1,2,4,128]{4,3,2,1,0:T(4,128)S(1)}, f32[1,1,2,4,128]{4,3,2,1,0:T(4,128)S(1)}, u32[]{:S(2)}, u32[]{:S(2)}) collective-permute-start(f32[1,1,2,4,128]{4,3,2,1,0:T(4,128)S(1)} %slice.2833), channel_id=1, source_target_pairs={{0,224},{32,0},{64,32},{96,64},{128,96},{160,128},{192,160},{224,1... | collective-permute-start | bytes 12296 | tf_op jit(solution)/shard_map/ppermute | solution.py:34
  71.2 3.7 %collective-permute-start.7 = (f32[1,3,1,4,128]{4,3,2,1,0:T(4,128)S(1)}, f32[1,3,1,4,128]{4,3,2,1,0:T(4,128)S(1)}, u32[]{:S(2)}, u32[]{:S(2)}) collective-permute-start(f32[1,3,1,4,128]{4,3,2,1,0:T(4,128)S(1)} %pad_maximum_fusion.21), channel_id=1, source_target_pairs={{0,28},{4,0},{8,4},{12,8},{16,12},{20,16},{24,20},{28,24},{1,29},{... | collective-permute-start | bytes 18440 | tf_op jit(solution)/shard_map/ppermute | solution.py:34
  79.1 6.5 %collective-permute-start.8 = (f32[1,3,3,1,128]{4,3,2,1,0:T(1,128)S(1)}, f32[1,3,3,1,128]{4,3,2,1,0:T(1,128)S(1)}, u32[]{:S(2)}, u32[]{:S(2)}) collective-permute-start(f32[1,3,3,1,128]{4,3,2,1,0:T(1,128)S(1)} %pad_maximum_fusion.22), channel_id=1, source_target_pairs={{0,3},{1,0},{2,1},{3,2},{4,7},{5,4},{6,5},{7,6},{8,11},{9,8},{10,9... | collective-permute-start | bytes 13832 | tf_op jit(solution)/shard_map/ppermute | solution.py:34
  129.6 14.8 %copy-start.14 = (f32[3,2,2,4,128]{4,3,2,1,0:T(4,128)S(1)}, f32[3,2,2,4,128]{4,3,2,1,0:T(4,128)}, u32[]{:S(2)}) copy-start(f32[3,2,2,4,128]{4,3,2,1,0:T(4,128)} %param.208) | copy-start | bytes 73732
  129.9 5.0 %collective-permute-start.9 = (f32[3,3,3,1,128]{4,3,2,1,0:T(1,128)S(1)}, f32[3,3,3,1,128]{4,3,2,1,0:T(1,128)S(1)}, u32[]{:S(2)}, u32[]{:S(2)}) collective-permute-start(f32[3,3,3,1,128]{4,3,2,1,0:T(1,128)S(1)} %slice.2863), channel_id=1, source_target_pairs={{0,1},{1,2},{2,3},{3,0},{4,5},{5,6},{6,7},{7,4},{8,9},{9,10},{10,1... | collective-permute-start | bytes 41480 | tf_op jit(solution)/shard_map/ppermute | solution.py:34
  135.0 5.0 %collective-permute-start.10 = (f32[3,3,1,4,128]{4,3,2,1,0:T(4,128)S(1)}, f32[3,3,1,4,128]{4,3,2,1,0:T(4,128)S(1)}, u32[]{:S(2)}, u32[]{:S(2)}) collective-permute-start(f32[3,3,1,4,128]{4,3,2,1,0:T(4,128)S(1)} %slice.2866), channel_id=1, source_target_pairs={{0,4},{4,8},{8,12},{12,16},{16,20},{20,24},{24,28},{28,0},{1,5},{5... | collective-permute-start | bytes 55304 | tf_op jit(solution)/shard_map/ppermute | solution.py:34
  140.1 4.3 %collective-permute-start.11 = (f32[3,1,2,4,128]{4,3,2,1,0:T(4,128)S(1)}, f32[3,1,2,4,128]{4,3,2,1,0:T(4,128)S(1)}, u32[]{:S(2)}, u32[]{:S(2)}) collective-permute-start(f32[3,1,2,4,128]{4,3,2,1,0:T(4,128)S(1)} %slice.2869), channel_id=1, source_target_pairs={{0,32},{32,64},{64,96},{96,128},{128,160},{160,192},{192,224},{224... | collective-permute-start | bytes 36872 | tf_op jit(solution)/shard_map/ppermute | solution.py:34
where the time goes:
time: 148 us; the launch traced here: 146 us
  other arithmetic  82.8 us (56%)
  waiting for transfers between devices  32.6 us (22%)
  starting transfers between devices  13.3 us (9%)
  local copies, waits for them, and re-layouts  8.28 us (6%)
  loops' own time  5.93 us (4%)
  between operations  2.64 us (2%)
    ppermute x12, waiting for transfers between devices, from_behind(): return lax.ppermute(value, axis, pairs)  32.6 us
    reduce_sum x28, other arithmetic, pair_force(): return (jnp.sum(pushed, axis=3), -jnp.sum(pushed, axis=2))  26.5 us
    mul x28, other arithmetic, pair_force(): tile_weight(mask_a, mask_b, self_tile) * 2.0  13.6 us
    reduce_sum x28, other arithmetic, pair_density(): radius_sq = jnp.sum(separation * separation, axis=0)  13.3 us
    reduce_sum x28, other arithmetic, pair_force(): radius_sq = jnp.sum(separation * separation, axis=0)  13.3 us
    ppermute x12, starting transfers between devices, from_behind(): return lax.ppermute(value, axis, pairs)  13.3 us
    reduce_sum x28, other arithmetic, pair_density(): return (jnp.sum(pair_term, axis=2), jnp.sum(pair_term, axis=1))  10.9 us
    dynamic_slice x268, local copies, waits for them, and re-layouts, take_cells(): return lax.dynamic_slice_in_dim(field, first_cell, block_size, axis_index)  4.17 us
  transfers between devices with their start and end apart: 12, of which 9 were waited for; matrix products, arithmetic and copies ran while one was open for 8% of the time, Pallas kernels for 0%

commit v1 on v0

v1 whole, which is shorter than its diff:
```python
import functools
import math

import jax
import jax.numpy as jnp
from jax import lax
from jax.experimental import pallas as pl
from jax.experimental.pallas import tpu as pltpu
from jax.sharding import PartitionSpec as P

MESH = pl.DeviceIdType.MESH
EDGE = 11.0
BETA = math.log2(math.e) / 4.0
ALPHA = 25.0 * BETA
DEAD = -30000.0
RHO_SHIFT = 8.0 * ALPHA / 25.0
PAIR_SHIFT = 4.0 * ALPHA / 25.0
RHO_SCALE = 0.4 * 2.0 ** (-ALPHA) / ALPHA**2
RHO_SLOPE_SCALE = -0.1 * 2.0 ** (-ALPHA) / ALPHA**2
PAIR_SLOPE_SCALE = -0.15 * 2.0 ** (-2.0 * ALPHA) / ALPHA**2
TIME_STEP = 0.5
OFFSETS = [
    (dx, dy, dz)
    for dx in (-1, 0, 1)
    for dy in (-1, 0, 1)
    for dz in (-1, 0, 1)
    if (dx, dy, dz) != (0, 0, 0)
]
OWN = (2, 2, 4)
EXT = (4, 4, 6)
CELLS = OWN[0] * OWN[1] * OWN[2]
EXT_CELLS = EXT[0] * EXT[1] * EXT[2]
F32, BF16 = jnp.float32, jnp.bfloat16


def source_slice(step, size):
    if step == 0:
        return pl.ds(1, size)
    return pl.ds(size if step > 0 else 1, 1)


def target_slice(step, size):
    if step == 0:
        return pl.ds(1, size)
    return pl.ds(0 if step > 0 else size + 1, 1)


def round16(value):
    return value.astype(BF16).astype(F32)


def split3(value):
    high = round16(value)
    rest = value - high
    low = round16(rest)
    return high, low, rest - low


def kernel(
    pos_ref, vel_ref, cnt_ref, vout_ref, mout_ref,
    ext, gext, lhs, mom, gmom, wts, accp, slopes,
    send_sem, recv_sem, gsend_sem, grecv_sem,
):
    sizes = [lax.axis_size(name) for name in ("gx", "gy", "gz")]
    me = [lax.axis_index(name) for name in ("gx", "gy", "gz")]

    def neighbour(offset):
        return tuple(lax.rem(m + d + n, n) for m, d, n in zip(me, offset, sizes))

    barrier = pltpu.get_barrier_semaphore()
    for offset in OFFSETS:
        pl.semaphore_signal(barrier, inc=1, device_id=neighbour(offset), device_id_type=MESH)

    lane = lax.broadcasted_iota(jnp.int32, (1, 128), 1)
    for x in range(OWN[0]):
        for y in range(OWN[1]):
            for z in range(OWN[2]):
                for c in range(3):
                    ext[1 + x, 1 + y, 1 + z, c : c + 1, :] = (
                        pos_ref[c, x, y, z : z + 1, :] - 0.5 * EDGE
                    )
                live = jnp.where(lane < cnt_ref[x, y, z], 1.0, 0.0)
                ext[1 + x, 1 + y, 1 + z, 3:4, :] = live

    pl.semaphore_wait(barrier, len(OFFSETS))

    def exchange(buffer, sends, recvs):
        copies = []
        for k, offset in enumerate(OFFSETS):
            src = tuple(source_slice(d, n) for d, n in zip(offset, OWN))
            dst = tuple(target_slice(d, n) for d, n in zip(offset, OWN))
            copy = pltpu.make_async_remote_copy(
                src_ref=buffer.at[src],
                dst_ref=buffer.at[dst],
                send_sem=sends.at[k],
                recv_sem=recvs.at[k],
                device_id=neighbour(offset),
                device_id_type=MESH,
            )
            copy.start()
            copies.append(copy)
        return copies

    copies = exchange(ext, send_sem, recv_sem)
    row4 = lax.broadcasted_iota(jnp.int32, (4, 128), 0)

    def shifted(x, y, z):
        cx = (x.astype(F32) - 1.5) * EDGE
        cy = (y.astype(F32) - 1.5) * EDGE
        cz = (z.astype(F32) - 2.5) * EDGE
        centre = jnp.where(row4 == 0, cx, jnp.where(row4 == 1, cy, jnp.where(row4 == 2, cz, 0.0)))
        return ext[x, y, z] + centre

    def norm_of(point):
        square = point * point
        total = square[0:1] + square[1:2] + square[2:3]
        return jnp.where(point[3:4] > 0.5, -BETA * total, DEAD)

    def own_step(i, carry):
        x, y, z = i // 8, lax.rem(i // 4, 2), lax.rem(i, 4)
        point = shifted(x + 1, y + 1, z + 1)
        high, low, rest = split3(jnp.where(row4 == 3, 1.0, (2.0 * BETA) * point))
        n_high, n_low, n_rest = split3(norm_of(point) + ALPHA)
        norm = jnp.where(row4 == 0, n_high, jnp.where(row4 == 1, n_low, jnp.where(row4 == 2, n_rest, 0.0)))
        wts[i] = jnp.concatenate(
            [high, low, rest, high, low, high, norm, jnp.zeros_like(norm)], axis=0
        ).astype(BF16)
        return carry

    lax.fori_loop(0, CELLS, own_step, 0)

    for copy in copies:
        copy.wait()

    def expand_step(j, carry):
        x, y, z = j // 24, lax.rem(j // 6, 4), lax.rem(j, 6)
        point = shifted(x, y, z)
        full = jnp.where(row4 == 3, norm_of(point), point)
        high, low, rest = split3(full)
        ones = jnp.ones_like(high)
        stack = jnp.concatenate([high, high, high, low, low, rest, ones, jnp.zeros_like(ones)], axis=0)
        lhs[j] = stack.T.astype(BF16)
        moments = jnp.concatenate([high, low, rest, ones], axis=0).astype(BF16)
        mom[j] = jnp.concatenate([moments, moments], axis=1)
        return carry

    lax.fori_loop(0, EXT_CELLS, expand_step, 0)

    eye = lax.broadcasted_iota(jnp.int32, (128, 128), 0) == lax.broadcasted_iota(jnp.int32, (128, 128), 1)

    def cell_base(i):
        return i // 8, lax.rem(i // 4, 2), lax.rem(i, 4)

    def pair_step(i, carry):
        x, y, z = cell_base(i)
        weight = wts[i]
        total = jnp.zeros((8, 128), F32)
        push = jnp.zeros((16, 128), F32)
        for k in range(27):
            dx, dy, dz = k // 9, k // 3 % 3, k % 3
            j = ((x + dx) * 4 + (y + dy)) * 6 + z + dz
            t = jnp.dot(lhs[j], weight, preferred_element_type=F32)
            remain = jnp.maximum(t, 0.0)
            if k == 13:
                remain = jnp.where(eye, 0.0, remain)
            fall = jnp.exp2(t)
            part = remain * fall
            rho = part * remain
            total = total + jnp.sum(rho.reshape(16, 8, 128), axis=0)
            slope = part * (remain + RHO_SHIFT)
            high = slope.astype(BF16)
            slopes[i * 27 + k, 0:128, :] = high
            slopes[i * 27 + k, 128:256, :] = (slope - high.astype(F32)).astype(BF16)
            pair = (part * fall) * (remain + PAIR_SHIFT)
            high = pair.astype(BF16)
            low = (pair - high.astype(F32)).astype(BF16)
            push = push + jnp.dot(
                mom[j], jnp.concatenate([high, low], axis=0), preferred_element_type=F32
            )
        density = RHO_SCALE * jnp.sum(total, axis=0, keepdims=True)
        live = ext[x + 1, y + 1, z + 1, 3:4, :]
        gext[x + 1, y + 1, z + 1] = live * 2.0 * (density - 1.0)
        accp[i] = push
        return carry

    lax.fori_loop(0, CELLS, pair_step, 0)

    copies = exchange(gext, gsend_sem, grecv_sem)
    for copy in copies:
        copy.wait()

    def grad_step(j, carry):
        x, y, z = j // 24, lax.rem(j // 6, 4), lax.rem(j, 6)
        point = jnp.where(row4 == 3, 1.0, shifted(x, y, z))
        high, low, rest = split3(point * gext[x, y, z])
        moments = jnp.concatenate([high, low, rest, jnp.zeros_like(rest)], axis=0).astype(BF16)
        gmom[j, 0:16, :] = mom[j]
        gmom[j, 16:32, :] = jnp.concatenate([moments, moments], axis=1)
        return carry

    lax.fori_loop(0, EXT_CELLS, grad_step, 0)

    def force_step(i, carry):
        x, y, z = cell_base(i)
        total = jnp.zeros((32, 128), F32)
        for k in range(27):
            dx, dy, dz = k // 9, k // 3 % 3, k % 3
            j = ((x + dx) * 4 + (y + dy)) * 6 + z + dz
            total = total + jnp.dot(gmom[j], slopes[i * 27 + k], preferred_element_type=F32)
        push = accp[i]
        point = shifted(x + 1, y + 1, z + 1)
        grad = gext[x + 1, y + 1, z + 1]
        live = point[3:4]

        def net(block, count):
            return block[0:4] + block[4:8] + block[8:12] - point * count

        pair_part = net(push, push[12:13])
        own_part = net(total[0:16], total[12:13])
        block = total[16:32]
        other_part = net(block, block[3:4] + block[7:8] + block[11:12])
        force = 2.0 * (
            PAIR_SLOPE_SCALE * pair_part + RHO_SLOPE_SCALE * (grad * own_part + other_part)
        )
        for c in range(3):
            place = pos_ref[c, x, y, pl.ds(z, 1), :]
            velocity = vel_ref[c, x, y, pl.ds(z, 1), :] + TIME_STEP * force[c : c + 1]
            vout_ref[c, x, y, pl.ds(z, 1), :] = velocity * live
            mout_ref[c, x, y, pl.ds(z, 1), :] = ((place + TIME_STEP * velocity) - place) * live
        return carry

    lax.fori_loop(0, CELLS, force_step, 0)


def body(positions, velocities, counts):
    vmem = pl.BlockSpec(memory_space=pltpu.VMEM)
    shape = jax.ShapeDtypeStruct(positions.shape, F32)
    links = len(OFFSETS)
    return pl.pallas_call(
        kernel,
        out_shape=(shape, shape),
        in_specs=[vmem, vmem, pl.BlockSpec(memory_space=pltpu.SMEM)],
        out_specs=(vmem, vmem),
        scratch_shapes=[
            pltpu.VMEM(EXT + (4, 128), F32),
            pltpu.VMEM(EXT + (1, 128), F32),
            pltpu.VMEM((EXT_CELLS, 128, 32), BF16),
            pltpu.VMEM((EXT_CELLS, 16, 256), BF16),
            pltpu.VMEM((EXT_CELLS, 32, 256), BF16),
            pltpu.VMEM((CELLS, 32, 128), BF16),
            pltpu.VMEM((CELLS, 16, 128), F32),
            pltpu.VMEM((CELLS * 27, 256, 128), BF16),
            pltpu.SemaphoreType.DMA((links,)),
            pltpu.SemaphoreType.DMA((links,)),
            pltpu.SemaphoreType.DMA((links,)),
            pltpu.SemaphoreType.DMA((links,)),
        ],
        compiler_params=pltpu.CompilerParams(
            collective_id=0, has_side_effects=True, vmem_limit_bytes=48 * 1024 * 1024
        ),
    )(positions, velocities, counts)


def solution(mesh):
    spec = P(None, "gx", "gy", "gz", None)
    return jax.shard_map(
        body,
        mesh=mesh,
        in_specs=(spec, spec, P("gx", "gy", "gz")),
        out_specs=(spec, spec),
        check_vma=False,
    )
```

time: 148 us -> 68.4 us (0.46)
  the two profiles are of different devices: /device:TPU:0 before, /device:TPU:1 now
where the time goes in v1:
time: 68.4 us; the launch traced here: 68.1 us
  Pallas kernels  64.1 us (94%)
  local copies, waits for them, and re-layouts  3.37 us (5%)
    pallas_call x1, Pallas kernels, body(): pl.pallas_call(kernel, out_shape=(shape, shape), in_specs=[vmem, vmem, pl...  64.1 us
    unnamed x8, local copies, waits for them, and re-layouts  3.37 us

profile of v1, /device:TPU:1, one launch (start us, length us, event | category | flops | bytes accessed | tf_op | source)
XLA Modules:
  0.0 68.1 jit_solution(2563750148664362396)
XLA Ops:
  0.6 0.0 copy-start
  0.6 0.7 %copy-done = f32[3,2,2,4,128]{4,3,2,1,0:T(4,128)S(1)} copy-done((f32[3,2,2,4,128]{4,3,2,1,0:T(4,128)S(1)}, f32[3,2,2,4,128]{4,3,2,1,0:T(4,128)}, u32[]{:S(2)}) %copy-start) | copy-done | bytes 24600
  1.4 0.0 copy-start.1
  1.4 0.7 %copy-done.1 = f32[3,2,2,4,128]{4,3,2,1,0:T(4,128)S(1)} copy-done((f32[3,2,2,4,128]{4,3,2,1,0:T(4,128)S(1)}, f32[3,2,2,4,128]{4,3,2,1,0:T(4,128)}, u32[]{:S(2)}) %copy-start.1) | copy-done | bytes 24600
  2.1 0.0 copy-start.2
  2.1 0.7 copy-done.2
  2.8 64.1 %shard_map.50 = (f32[3,2,2,4,128]{4,3,2,1,0:T(4,128)S(1)}, f32[3,2,2,4,128]{4,3,2,1,0:T(4,128)S(1)}) custom-call(f32[3,2,2,4,128]{4,3,2,1,0:T(4,128)S(1)} %copy-done, f32[3,2,2,4,128]{4,3,2,1,0:T(4,128)S(1)} %copy-done.1, s32[2,2,4]{2,1,0:T(2,128)S(1)} %copy-done.2), custom_call_target="tpu_custom_call" | custom-call | tf_op jit(solution)/shard_map/pallas_call | solution.py:239
  66.9 0.6 copy.7
  67.5 0.6 copy.8
Async XLA Ops:
  0.6 0.7 %copy-start = (f32[3,2,2,4,128]{4,3,2,1,0:T(4,128)S(1)}, f32[3,2,2,4,128]{4,3,2,1,0:T(4,128)}, u32[]{:S(2)}) copy-start(f32[3,2,2,4,128]{4,3,2,1,0:T(4,128)} %pos_ref.1) | copy-start | bytes 73732
  1.4 0.7 %copy-start.1 = (f32[3,2,2,4,128]{4,3,2,1,0:T(4,128)S(1)}, f32[3,2,2,4,128]{4,3,2,1,0:T(4,128)}, u32[]{:S(2)}) copy-start(f32[3,2,2,4,128]{4,3,2,1,0:T(4,128)} %vel_ref.1) | copy-start | bytes 73732
  2.1 0.7 %copy-start.2 = (s32[2,2,4]{2,1,0:T(2,128)S(1)}, s32[2,2,4]{2,1,0:T(2,128)}, u32[]{:S(2)}) copy-start(s32[2,2,4]{2,1,0:T(2,128)} %cnt_ref.1) | copy-start | bytes 196

commit v2 on v1

v2 whole, which is shorter than its diff:
```python
import functools
import math

import jax
import jax.numpy as jnp
from jax import lax
from jax.experimental import pallas as pl
from jax.experimental.pallas import tpu as pltpu
from jax.sharding import PartitionSpec as P

MESH = pl.DeviceIdType.MESH
EDGE = 11.0
BETA = math.log2(math.e) / 4.0
ALPHA = 25.0 * BETA
DEAD = -30000.0
SHIFT = 4.0 * ALPHA / 25.0
RHO_SCALE = 0.4 * 2.0 ** (-ALPHA) / ALPHA**2
FORCE_SCALE = 2.0 * -0.15 * 2.0 ** (-2.0 * ALPHA) / ALPHA**2
GRAD_SCALE = 2.0 / 3.0 * 2.0**ALPHA
TIME_STEP = 0.5
OFFSETS = [
    (dx, dy, dz)
    for dx in (-1, 0, 1)
    for dy in (-1, 0, 1)
    for dz in (-1, 0, 1)
    if (dx, dy, dz) != (0, 0, 0)
]
OWN = (2, 2, 4)
EXT = (4, 4, 6)
CELLS = OWN[0] * OWN[1] * OWN[2]
COLUMNS = EXT[0] * EXT[1]
GRAD_ROWS = 8 * EXT[2]
F32, BF16 = jnp.float32, jnp.bfloat16


def source_slice(step, size):
    if step == 0:
        return pl.ds(1, size)
    return pl.ds(size if step > 0 else 1, 1)


def target_slice(step, size):
    if step == 0:
        return pl.ds(1, size)
    return pl.ds(0 if step > 0 else size + 1, 1)


def round16(value):
    return value.astype(BF16).astype(F32)


def split3(value):
    high = round16(value)
    rest = value - high
    low = round16(rest)
    return high, low, rest - low


def kernel(
    pos_hbm, vel_hbm, cnt_hbm, vout_ref, mout_ref,
    pos_ref, vel_ref, cnt_ref, ext, gext, lhs, mom, wts, pwts, gwide, grow, wide, single, dens, push,
    load_sem, send_sem, recv_sem, gsend_sem, grecv_sem,
):
    loads = [
        pltpu.make_async_copy(source, target, load_sem.at[k])
        for k, (source, target) in enumerate(
            ((pos_hbm, pos_ref), (cnt_hbm, cnt_ref), (vel_hbm, vel_ref))
        )
    ]
    for load in loads:
        load.start()

    sizes = [lax.axis_size(name) for name in ("gx", "gy", "gz")]
    me = [lax.axis_index(name) for name in ("gx", "gy", "gz")]

    def neighbour(offset):
        return tuple(lax.rem(m + d + n, n) for m, d, n in zip(me, offset, sizes))

    barrier = pltpu.get_barrier_semaphore()
    for offset in OFFSETS:
        pl.semaphore_signal(barrier, inc=1, device_id=neighbour(offset), device_id_type=MESH)

    for load in loads:
        load.wait()
    lane = lax.broadcasted_iota(jnp.int32, (1, 128), 1)
    for x in range(OWN[0]):
        for y in range(OWN[1]):
            for z in range(OWN[2]):
                for c in range(3):
                    ext[1 + x, 1 + y, 1 + z, c : c + 1, :] = (
                        pos_ref[c, x, y, z : z + 1, :] - 0.5 * EDGE
                    )
                live = jnp.where(lane < cnt_ref[x, y, z], 1.0, 0.0)
                ext[1 + x, 1 + y, 1 + z, 3:4, :] = live

    pl.semaphore_wait(barrier, len(OFFSETS))

    def exchange(buffer, sends, recvs):
        copies = []
        for k, offset in enumerate(OFFSETS):
            src = tuple(source_slice(d, n) for d, n in zip(offset, OWN))
            dst = tuple(target_slice(d, n) for d, n in zip(offset, OWN))
            copy = pltpu.make_async_remote_copy(
                src_ref=buffer.at[src],
                dst_ref=buffer.at[dst],
                send_sem=sends.at[k],
                recv_sem=recvs.at[k],
                device_id=neighbour(offset),
                device_id_type=MESH,
            )
            copy.start()
            copies.append(copy)
        return copies

    copies = exchange(ext, send_sem, recv_sem)
    row4 = lax.broadcasted_iota(jnp.int32, (4, 128), 0)

    def by_row(values):
        result = jnp.zeros((4, 128), F32)
        for k, value in enumerate(values):
            result = jnp.where(row4 == k, value, result)
        return result

    def shifted(x, y, z):
        cx = (x.astype(F32) - 1.5) * EDGE
        cy = (y.astype(F32) - 1.5) * EDGE
        cz = (z - 2.5) * EDGE
        return ext[x, y, z] + by_row((cx, cy, cz))

    def norm_of(point):
        square = point * point
        total = square[0:1] + square[1:2] + square[2:3]
        return jnp.where(point[3:4] > 0.5, -BETA * total, DEAD)

    def expand(x, y, z):
        point = shifted(x, y, z)
        norm = norm_of(point)
        high, low, rest = split3(jnp.where(row4 == 3, norm, point))
        ones = jnp.ones_like(high)
        stack = jnp.concatenate([high, high, high, low, low, rest, ones, jnp.zeros_like(ones)], axis=0)
        j = (x * 4 + y, z)
        lhs[j] = stack.T.astype(BF16)
        moments = jnp.concatenate([high, low, rest, ones], axis=0).astype(BF16)
        mom[j] = jnp.concatenate([moments, moments], axis=1)
        return point, norm

    def pair_columns(k):
        side = lax.rem(k, 2)
        return jnp.where(k < 2, 2 * side, side), jnp.where(k < 2, 2 * side + 1, side + 2)

    def own_column(q):
        return 1 + q // 2, 1 + lax.rem(q, 2)

    def own_step(q, carry):
        x, y = own_column(q)
        for z in range(4):
            point, norm = expand(x, y, z + 1)
            high, low, rest = split3(jnp.where(row4 == 3, 1.0, (2.0 * BETA) * point))
            pieces = by_row(split3(norm + ALPHA))
            wts[q * 4 + z] = jnp.concatenate(
                [high, low, rest, high, low, high, pieces, jnp.zeros_like(pieces)], axis=0
            ).astype(BF16)
        return carry

    lax.fori_loop(0, 4, own_step, 0)

    def pair_step(k, carry):
        first, second = pair_columns(k)
        for z in range(4):
            pwts[k * 4 + z] = jnp.concatenate([wts[first * 4 + z], wts[second * 4 + z]], axis=1)
        return carry

    lax.fori_loop(0, 4, pair_step, 0)

    eye = lax.broadcasted_iota(jnp.int32, (128, 128), 0) == lax.broadcasted_iota(jnp.int32, (128, 128), 1)
    own_pairs = [(iz, jz) for iz in range(4) for jz in range(1, 5) if abs(iz + 1 - jz) <= 1]
    edge_pairs = [(0, 0), (3, 5)]
    all_pairs = [(iz, iz + dz) for iz in range(4) for dz in range(3)]

    def density_tile(j, weight, masked, store, slot):
        t = jnp.dot(lhs[j], weight, preferred_element_type=F32)
        width = t.shape[1]
        remain = jnp.maximum(t, 0.0)
        if masked is not None:
            halves = [remain[:, h * 128 : h * 128 + 128] for h in range(width // 128)]
            halves[masked] = jnp.where(eye, 0.0, halves[masked])
            remain = jnp.concatenate(halves, axis=1)
        part = remain * jnp.exp2(t)
        store[slot] = part
        return jnp.sum((part * remain).reshape(16, 8, width), axis=0)

    def force_tile(j, weight, grad, store, slot):
        t = jnp.dot(lhs[j], weight, preferred_element_type=F32)
        width = t.shape[1]
        column, z = j
        other = gwide[column, :, z * 128 : z * 128 + 128]
        if width == 256:
            other = jnp.concatenate([other, other], axis=1)
        both = other + grad
        factor = store[slot] * ((t + SHIFT) * (jnp.exp2(t) + both) + SHIFT * both)
        high = factor.astype(BF16)
        low = (factor - high.astype(F32)).astype(BF16)
        return jnp.dot(mom[j], jnp.concatenate([high, low], axis=0), preferred_element_type=F32)

    def group(kind, bases, weights, items, store, slot, first=False):
        totals = {}
        for n, (column, iz, jz, masked) in enumerate(items):
            j = (column, jz)
            weight = weights(iz)
            if kind == "density":
                part = density_tile(j, weight, masked, store, slot + n)
            else:
                grad = jnp.concatenate([grow[base + iz] for base in bases], axis=1)
                part = force_tile(j, weight, grad, store, slot + n)
            totals[iz] = part if iz not in totals else totals[iz] + part
        target = dens if kind == "density" else push
        for iz, total in totals.items():
            for h, base in enumerate(bases):
                block = total[:, h * 128 : h * 128 + 128]
                target[base + iz] = block if first else target[base + iz] + block

    def pair_group(kind, k, items, slot, first=False):
        one, two = pair_columns(k)
        group(kind, [one * 4, two * 4], lambda iz: pwts[k * 4 + iz], items, wide, slot, first)

    def own_part(kind):
        def same_step(k, carry):
            columns = [(1 + k) * 4 + y for y in (1, 2)]
            items = [
                (column, iz, jz, h if jz == iz + 1 else None)
                for h, column in enumerate(columns)
                for iz, jz in own_pairs
            ]
            pair_group(kind, k, items, k * 20, True)
            return carry

        def other_step(p, carry):
            k = p // 2
            column = (2 - k) * 4 + 1 + lax.rem(p, 2)
            pair_group(kind, k, [(column, iz, jz, None) for iz, jz in own_pairs], 40 + p * 10)
            return carry

        lax.fori_loop(0, 2, same_step, 0)
        lax.fori_loop(0, 4, other_step, 0)

    def halo_part(kind):
        def edge_step(k, carry):
            items = [(c, iz, jz, None) for c in (5, 6, 9, 10) for iz, jz in edge_pairs]
            pair_group(kind, k, items, 80 + k * 8)
            return carry

        def face_step(p, carry):
            k, far = p // 2, lax.rem(p, 2)
            side = 1 + lax.rem(k, 2)
            near = k < 2
            column = jnp.where(near, 4 * (3 * (side - 1)) + 1 + far, 4 * (1 + far) + 3 * (side - 1))
            pair_group(kind, k, [(column, iz, jz, None) for iz, jz in all_pairs], 96 + p * 12)
            return carry

        def corner_step(q, carry):
            column = 12 * (q // 2) + 3 * lax.rem(q, 2)
            group(
                kind, [q * 4], lambda iz: wts[q * 4 + iz],
                [(column, iz, jz, None) for iz, jz in all_pairs], single, q * 12,
            )
            return carry

        lax.fori_loop(0, 2, edge_step, 0)
        lax.fori_loop(0, 8, face_step, 0)
        lax.fori_loop(0, 4, corner_step, 0)

    def halo_column(k):
        x = jnp.where(k < 4, 0, jnp.where(k < 8, 3, 1 + lax.rem(k, 2)))
        y = jnp.where(k < 8, lax.rem(k, 4), jnp.where(k < 10, 0, 3))
        return x, y

    own_part("density")

    for copy in copies:
        copy.wait()

    def halo_expand(k, carry):
        x, y = halo_column(k)
        for z in range(6):
            expand(x, y, z)
        return carry

    def edge_expand(q, carry):
        x, y = own_column(q)
        expand(x, y, 0)
        expand(x, y, 5)
        return carry

    lax.fori_loop(0, 4, edge_expand, 0)
    lax.fori_loop(0, 12, halo_expand, 0)

    halo_part("density")

    def grad_step(q, carry):
        x, y = own_column(q)
        for z in range(4):
            density = RHO_SCALE * jnp.sum(dens[q * 4 + z], axis=0, keepdims=True)
            gext[x, y, z + 1] = ext[x, y, z + 1, 3:4, :] * 2.0 * (density - 1.0)
        return carry

    lax.fori_loop(0, 4, grad_step, 0)
    copies = exchange(gext, gsend_sem, grecv_sem)

    row8 = lax.broadcasted_iota(jnp.int32, (8, 128), 0)

    def grad_column(x, y, inner):
        rows = []
        for z in range(6):
            if inner and z in (0, 5):
                rows.append(jnp.zeros((8, 128), F32))
                continue
            high, low, rest = split3(GRAD_SCALE * gext[x, y, z])
            rows.append(
                jnp.where(row8 == 0, high, jnp.where(row8 == 1, low, jnp.where(row8 == 2, rest, 0.0)))
            )
        turned = jnp.concatenate(rows, axis=0).T.astype(BF16)
        gwide[x * 4 + y] = jnp.dot(turned, spread, preferred_element_type=F32)

    spread_row = lax.broadcasted_iota(jnp.int32, (GRAD_ROWS, 768), 0) // 8
    spread_lane = lax.broadcasted_iota(jnp.int32, (GRAD_ROWS, 768), 1) // 128
    spread = jnp.where(spread_row == spread_lane, 1.0, 0.0).astype(BF16)

    def own_grad(q, carry):
        x, y = own_column(q)
        for z in range(4):
            grow[q * 4 + z] = GRAD_SCALE * gext[x, y, z + 1]
        grad_column(x, y, True)
        return carry

    lax.fori_loop(0, 4, own_grad, 0)

    own_part("force")

    for copy in copies:
        copy.wait()

    def halo_grad(k, carry):
        x, y = halo_column(k)
        grad_column(x, y, False)
        return carry

    def edge_grad(q, carry):
        x, y = own_column(q)
        grad_column(x, y, False)
        return carry

    lax.fori_loop(0, 4, edge_grad, 0)
    lax.fori_loop(0, 12, halo_grad, 0)

    halo_part("force")

    def finish(q, carry):
        x, y = own_column(q)
        for z in range(4):
            total = push[q * 4 + z]
            point = shifted(x, y, z + 1)
            live = point[3:4]
            force = FORCE_SCALE * (total[0:4] + total[4:8] + total[8:12] - point * total[12:13])
            for c in range(3):
                place = pos_ref[c, x - 1, y - 1, z : z + 1, :]
                velocity = vel_ref[c, x - 1, y - 1, z : z + 1, :] + TIME_STEP * force[c : c + 1]
                vout_ref[c, x - 1, y - 1, z : z + 1, :] = velocity * live
                mout_ref[c, x - 1, y - 1, z : z + 1, :] = (
                    (place + TIME_STEP * velocity) - place
                ) * live
        return carry

    lax.fori_loop(0, 4, finish, 0)


def body(positions, velocities, counts):
    vmem = pl.BlockSpec(memory_space=pltpu.VMEM)
    hbm = pl.BlockSpec(memory_space=pltpu.HBM)
    shape = jax.ShapeDtypeStruct(positions.shape, F32)
    links = len(OFFSETS)
    return pl.pallas_call(
        kernel,
        out_shape=(shape, shape),
        in_specs=[hbm, hbm, hbm],
        out_specs=(vmem, vmem),
        scratch_shapes=[
            pltpu.VMEM(positions.shape, F32),
            pltpu.VMEM(positions.shape, F32),
            pltpu.SMEM(counts.shape, jnp.int32),
            pltpu.VMEM(EXT + (4, 128), F32),
            pltpu.VMEM(EXT + (1, 128), F32),
            pltpu.VMEM((COLUMNS, 6, 128, 32), BF16),
            pltpu.VMEM((COLUMNS, 6, 16, 256), BF16),
            pltpu.VMEM((CELLS, 32, 128), BF16),
            pltpu.VMEM((CELLS, 32, 256), BF16),
            pltpu.VMEM((COLUMNS, 128, 768), F32),
            pltpu.VMEM((CELLS, 1, 128), F32),
            pltpu.VMEM((192, 128, 256), F32),
            pltpu.VMEM((48, 128, 128), F32),
            pltpu.VMEM((CELLS, 8, 128), F32),
            pltpu.VMEM((CELLS, 16, 128), F32),
            pltpu.SemaphoreType.DMA((3,)),
            pltpu.SemaphoreType.DMA((links,)),
            pltpu.SemaphoreType.DMA((links,)),
            pltpu.SemaphoreType.DMA((links,)),
            pltpu.SemaphoreType.DMA((links,)),
        ],
        compiler_params=pltpu.CompilerParams(
            collective_id=0, has_side_effects=True, vmem_limit_bytes=56 * 1024 * 1024
        ),
    )(positions, velocities, counts)


def solution(mesh):
    spec = P(None, "gx", "gy", "gz", None)
    return jax.shard_map(
        body,
        mesh=mesh,
        in_specs=(spec, spec, P("gx", "gy", "gz")),
        out_specs=(spec, spec),
        check_vma=False,
    )
```

time: 68.4 us -> 54.3 us (0.79)
  Pallas kernels: 64.1 us -> 51.4 us
  local copies, waits for them, and re-layouts: 3.37 us -> 1.96 us
    pallas_call x1, Pallas kernels: 64.1 us -> 51.4 us  [body(): pl.pallas_call(kernel, out_shape=(shape, shape), in_specs=[hbm, hbm, hbm]...]
    unnamed x8 -> x4, local copies, waits for them, and re-layouts: 3.37 us -> 1.96 us
where the time goes in v2:
time: 54.3 us; the launch traced here: 54.1 us
  Pallas kernels  51.4 us (95%)
  local copies, waits for them, and re-layouts  1.96 us (4%)
  between operations  0.65 us (1%)
    pallas_call x1, Pallas kernels, body(): pl.pallas_call(kernel, out_shape=(shape, shape), in_specs=[hbm, hbm, hbm]...  51.4 us
    unnamed x4, local copies, waits for them, and re-layouts  1.96 us

profile of v2, /device:TPU:1, one launch (start us, length us, event | category | flops | bytes accessed | tf_op | source)
XLA Modules:
  0.0 54.1 jit_solution(1597745964365108045)
XLA Ops:
  0.6 51.4 %shard_map.50 = (f32[3,2,2,4,128]{4,3,2,1,0:T(4,128)}, f32[3,2,2,4,128]{4,3,2,1,0:T(4,128)}) custom-call(f32[3,2,2,4,128]{4,3,2,1,0:T(4,128)} %pos_hbm.1, f32[3,2,2,4,128]{4,3,2,1,0:T(4,128)} %vel_hbm.1, s32[2,2,4]{2,1,0:T(2,128)} %cnt_hbm.1), custom_call_target="tpu_custom_call" | custom-call | tf_op jit(solution)/shard_map/pallas_call | solution.py:381
  52.1 0.0 copy-start
  52.1 1.4 %copy.7 = f32[3,2,2,4,128]{4,3,2,1,0:T(4,128)} copy(f32[3,2,2,4,128]{4,3,2,1,0:T(4,128)} %get-tuple-element.4) | data formatting | bytes 49152
  53.4 0.0 copy-done
  53.5 0.6 %copy.8 = f32[3,2,2,4,128]{4,3,2,1,0:T(4,128)} copy(f32[3,2,2,4,128]{4,3,2,1,0:T(4,128)S(1)} %copy-done) | data formatting | bytes 49152
Async XLA Ops:
  52.1 1.4 %copy-start = (f32[3,2,2,4,128]{4,3,2,1,0:T(4,128)S(1)}, f32[3,2,2,4,128]{4,3,2,1,0:T(4,128)}, u32[]{:S(2)}) copy-start(f32[3,2,2,4,128]{4,3,2,1,0:T(4,128)} %get-tuple-element.5) | copy-start | bytes 73732

commit v3 on v2

--- a/solution.py
+++ b/solution.py
@@ -10,13 +10,12 @@
 
 MESH = pl.DeviceIdType.MESH
 EDGE = 11.0
-BETA = math.log2(math.e) / 4.0
-ALPHA = 25.0 * BETA
+LOG2E = math.log2(math.e)
+PEAK = 25.0 / 4.0
 DEAD = -30000.0
-SHIFT = 4.0 * ALPHA / 25.0
-RHO_SCALE = 0.4 * 2.0 ** (-ALPHA) / ALPHA**2
-FORCE_SCALE = 2.0 * -0.15 * 2.0 ** (-2.0 * ALPHA) / ALPHA**2
-GRAD_SCALE = 2.0 / 3.0 * 2.0**ALPHA
+RHO_SCALE = 0.4 * math.exp(-PEAK) / PEAK**2
+FORCE_SCALE = 2.0 * -0.15 * math.exp(-2.0 * PEAK) / PEAK**2
+GRAD_SCALE = 2.0 / 3.0 * math.exp(PEAK)
 TIME_STEP = 0.5
 OFFSETS = [
     (dx, dy, dz)
@@ -58,7 +57,7 @@
 
 def kernel(
     pos_hbm, vel_hbm, cnt_hbm, vout_ref, mout_ref,
-    pos_ref, vel_ref, cnt_ref, ext, gext, lhs, mom, wts, pwts, gwide, grow, wide, single, dens, push,
+    pos_ref, vel_ref, cnt_ref, ext, gext, lhs, mom, wts, pwts, gwide, grow, own_part_a, wide_p, wide_r, single_p, single_r, dens, push,
     load_sem, send_sem, recv_sem, gsend_sem, grecv_sem,
 ):
     loads = [
@@ -122,15 +121,15 @@
         return result
 
     def shifted(x, y, z):
-        cx = (x.astype(F32) - 1.5) * EDGE
-        cy = (y.astype(F32) - 1.5) * EDGE
+        cx = (x - 1.5) * EDGE
+        cy = (y - 1.5) * EDGE
         cz = (z - 2.5) * EDGE
         return ext[x, y, z] + by_row((cx, cy, cz))
 
     def norm_of(point):
         square = point * point
         total = square[0:1] + square[1:2] + square[2:3]
-        return jnp.where(point[3:4] > 0.5, -BETA * total, DEAD)
+        return jnp.where(point[3:4] > 0.5, -0.25 * total, DEAD)
 
     def expand(x, y, z):
         point = shifted(x, y, z)
@@ -155,11 +154,16 @@
         x, y = own_column(q)
         for z in range(4):
             point, norm = expand(x, y, z + 1)
-            high, low, rest = split3(jnp.where(row4 == 3, 1.0, (2.0 * BETA) * point))
-            pieces = by_row(split3(norm + ALPHA))
-            wts[q * 4 + z] = jnp.concatenate(
-                [high, low, rest, high, low, high, pieces, jnp.zeros_like(pieces)], axis=0
-            ).astype(BF16)
+            blocks = []
+            for unit in (LOG2E, 1.0):
+                high, low, rest = split3(jnp.where(row4 == 3, unit, (0.5 * unit) * point))
+                pieces = by_row(split3(unit * (norm + PEAK)))
+                blocks.append(
+                    jnp.concatenate(
+                        [high, low, rest, high, low, high, pieces, jnp.zeros_like(pieces)], axis=0
+                    )
+                )
+            wts[q * 4 + z] = jnp.concatenate(blocks, axis=1).astype(BF16)
         return carry
 
     lax.fori_loop(0, 4, own_step, 0)
@@ -167,7 +171,10 @@
     def pair_step(k, carry):
         first, second = pair_columns(k)
         for z in range(4):
-            pwts[k * 4 + z] = jnp.concatenate([wts[first * 4 + z], wts[second * 4 + z]], axis=1)
+            one, two = wts[first * 4 + z], wts[second * 4 + z]
+            pwts[k * 4 + z] = jnp.concatenate(
+                [one[:, 0:128], two[:, 0:128], one[:, 128:256], two[:, 128:256]], axis=1
+            )
         return carry
 
     lax.fori_loop(0, 4, pair_step, 0)
@@ -177,41 +184,52 @@
     edge_pairs = [(0, 0), (3, 5)]
     all_pairs = [(iz, iz + dz) for iz in range(4) for dz in range(3)]
 
-    def density_tile(j, weight, masked, store, slot):
-        t = jnp.dot(lhs[j], weight, preferred_element_type=F32)
-        width = t.shape[1]
-        remain = jnp.maximum(t, 0.0)
+    def density_tile(j, weight, masked, stores, slot):
+        both = jnp.dot(lhs[j], weight, preferred_element_type=F32)
+        width = both.shape[1] // 2
+        fall = jnp.exp2(both[:, 0:width])
+        remain = jnp.maximum(both[:, width:], 0.0)
         if masked is not None:
             halves = [remain[:, h * 128 : h * 128 + 128] for h in range(width // 128)]
             halves[masked] = jnp.where(eye, 0.0, halves[masked])
             remain = jnp.concatenate(halves, axis=1)
-        part = remain * jnp.exp2(t)
-        store[slot] = part
-        return jnp.sum((part * remain).reshape(16, 8, width), axis=0)
-
-    def force_tile(j, weight, grad, store, slot):
-        t = jnp.dot(lhs[j], weight, preferred_element_type=F32)
-        width = t.shape[1]
+        part = remain * fall
+        rho = part * remain
+        if len(stores) == 1:
+            stores[0][slot] = part
+        else:
+            mixed = rho + part
+            stores[0][slot] = mixed * fall
+            stores[1][slot] = mixed + part
+        return jnp.sum(rho.reshape(16, 8, width), axis=0)
+
+    def force_tile(j, weight, grad, stores, slot):
+        width = grad.shape[1]
         column, z = j
         other = gwide[column, :, z * 128 : z * 128 + 128]
         if width == 256:
             other = jnp.concatenate([other, other], axis=1)
-        both = other + grad
-        factor = store[slot] * ((t + SHIFT) * (jnp.exp2(t) + both) + SHIFT * both)
+        sums = other + grad
+        if len(stores) == 1:
+            both = jnp.dot(lhs[j], weight, preferred_element_type=F32)
+            fall = jnp.exp2(both[:, 0:width])
+            factor = stores[0][slot] * ((both[:, width:] + 1.0) * (fall + sums) + sums)
+        else:
+            factor = stores[0][slot] + stores[1][slot] * sums
         high = factor.astype(BF16)
         low = (factor - high.astype(F32)).astype(BF16)
         return jnp.dot(mom[j], jnp.concatenate([high, low], axis=0), preferred_element_type=F32)
 
-    def group(kind, bases, weights, items, store, slot, first=False):
+    def group(kind, bases, weights, items, stores, slot, first=False):
         totals = {}
         for n, (column, iz, jz, masked) in enumerate(items):
             j = (column, jz)
             weight = weights(iz)
             if kind == "density":
-                part = density_tile(j, weight, masked, store, slot + n)
+                part = density_tile(j, weight, masked, stores, slot + n)
             else:
                 grad = jnp.concatenate([grow[base + iz] for base in bases], axis=1)
-                part = force_tile(j, weight, grad, store, slot + n)
+                part = force_tile(j, weight, grad, stores, slot + n)
             totals[iz] = part if iz not in totals else totals[iz] + part
         target = dens if kind == "density" else push
         for iz, total in totals.items():
@@ -219,9 +237,9 @@
                 block = total[:, h * 128 : h * 128 + 128]
                 target[base + iz] = block if first else target[base + iz] + block
 
-    def pair_group(kind, k, items, slot, first=False):
+    def pair_group(kind, k, items, stores, slot, first=False):
         one, two = pair_columns(k)
-        group(kind, [one * 4, two * 4], lambda iz: pwts[k * 4 + iz], items, wide, slot, first)
+        group(kind, [one * 4, two * 4], lambda iz: pwts[k * 4 + iz], items, stores, slot, first)
 
     def own_part(kind):
         def same_step(k, carry):
@@ -231,13 +249,13 @@
                 for h, column in enumerate(columns)
                 for iz, jz in own_pairs
             ]
-            pair_group(kind, k, items, k * 20, True)
+            pair_group(kind, k, items, [own_part_a], k * 20, True)
             return carry
 
         def other_step(p, carry):
             k = p // 2
             column = (2 - k) * 4 + 1 + lax.rem(p, 2)
-            pair_group(kind, k, [(column, iz, jz, None) for iz, jz in own_pairs], 40 + p * 10)
+            pair_group(kind, k, [(column, iz, jz, None) for iz, jz in own_pairs], [own_part_a], 40 + p * 10)
             return carry
 
         lax.fori_loop(0, 2, same_step, 0)
@@ -246,7 +264,7 @@
     def halo_part(kind):
         def edge_step(k, carry):
             items = [(c, iz, jz, None) for c in (5, 6, 9, 10) for iz, jz in edge_pairs]
-            pair_group(kind, k, items, 80 + k * 8)
+            pair_group(kind, k, items, [wide_p, wide_r], k * 8)
             return carry
 
         def face_step(p, carry):
@@ -254,14 +272,14 @@
             side = 1 + lax.rem(k, 2)
             near = k < 2
             column = jnp.where(near, 4 * (3 * (side - 1)) + 1 + far, 4 * (1 + far) + 3 * (side - 1))
-            pair_group(kind, k, [(column, iz, jz, None) for iz, jz in all_pairs], 96 + p * 12)
+            pair_group(kind, k, [(column, iz, jz, None) for iz, jz in all_pairs], [wide_p, wide_r], 16 + p * 12)
             return carry
 
         def corner_step(q, carry):
             column = 12 * (q // 2) + 3 * lax.rem(q, 2)
             group(
                 kind, [q * 4], lambda iz: wts[q * 4 + iz],
-                [(column, iz, jz, None) for iz, jz in all_pairs], single, q * 12,
+                [(column, iz, jz, None) for iz, jz in all_pairs], [single_p, single_r], q * 12,
             )
             return carry
 
@@ -280,19 +298,21 @@
         copy.wait()
 
     def halo_expand(k, carry):
-        x, y = halo_column(k)
-        for z in range(6):
-            expand(x, y, z)
+        for n in range(2):
+            x, y = halo_column(2 * k + n)
+            for z in range(6):
+                expand(x, y, z)
         return carry
 
     def edge_expand(q, carry):
-        x, y = own_column(q)
-        expand(x, y, 0)
-        expand(x, y, 5)
-        return carry
-
-    lax.fori_loop(0, 4, edge_expand, 0)
-    lax.fori_loop(0, 12, halo_expand, 0)
+        x = q + 1
+        for y in (1, 2):
+            expand(x, y, 0)
+            expand(x, y, 5)
+        return carry
+
+    lax.fori_loop(0, 2, edge_expand, 0)
+    lax.fori_loop(0, 6, halo_expand, 0)
 
     halo_part("density")
 
@@ -325,32 +345,22 @@
     spread_lane = lax.broadcasted_iota(jnp.int32, (GRAD_ROWS, 768), 1) // 128
     spread = jnp.where(spread_row == spread_lane, 1.0, 0.0).astype(BF16)
 
-    def own_grad(q, carry):
-        x, y = own_column(q)
+    for q in range(4):
         for z in range(4):
-            grow[q * 4 + z] = GRAD_SCALE * gext[x, y, z + 1]
-        grad_column(x, y, True)
-        return carry
-
-    lax.fori_loop(0, 4, own_grad, 0)
+            grow[q * 4 + z] = GRAD_SCALE * gext[1 + q // 2, 1 + q % 2, z + 1]
+        grad_column(1 + q // 2, 1 + q % 2, True)
 
     own_part("force")
 
     for copy in copies:
         copy.wait()
 
-    def halo_grad(k, carry):
-        x, y = halo_column(k)
-        grad_column(x, y, False)
-        return carry
-
-    def edge_grad(q, carry):
-        x, y = own_column(q)
-        grad_column(x, y, False)
-        return carry
-
-    lax.fori_loop(0, 4, edge_grad, 0)
-    lax.fori_loop(0, 12, halo_grad, 0)
+    def row_grad(x, carry):
+        for y in range(4):
+            grad_column(x, y, False)
+        return carry
+
+    lax.fori_loop(0, 4, row_grad, 0)
 
     halo_part("force")
 
@@ -391,11 +401,14 @@
             pltpu.VMEM(EXT + (1, 128), F32),
             pltpu.VMEM((COLUMNS, 6, 128, 32), BF16),
             pltpu.VMEM((COLUMNS, 6, 16, 256), BF16),
-            pltpu.VMEM((CELLS, 32, 128), BF16),
             pltpu.VMEM((CELLS, 32, 256), BF16),
+            pltpu.VMEM((CELLS, 32, 512), BF16),
             pltpu.VMEM((COLUMNS, 128, 768), F32),
             pltpu.VMEM((CELLS, 1, 128), F32),
-            pltpu.VMEM((192, 128, 256), F32),
+            pltpu.VMEM((80, 128, 256), F32),
+            pltpu.VMEM((112, 128, 256), F32),
+            pltpu.VMEM((112, 128, 256), F32),
+            pltpu.VMEM((48, 128, 128), F32),
             pltpu.VMEM((48, 128, 128), F32),
             pltpu.VMEM((CELLS, 8, 128), F32),
             pltpu.VMEM((CELLS, 16, 128), F32),
@@ -406,7 +419,7 @@
             pltpu.SemaphoreType.DMA((links,)),
         ],
         compiler_params=pltpu.CompilerParams(
-            collective_id=0, has_side_effects=True, vmem_limit_bytes=56 * 1024 * 1024
+            collective_id=0, has_side_effects=True, vmem_limit_bytes=60 * 1024 * 1024
         ),
     )(positions, velocities, counts)
 

time: 54.3 us -> 48.8 us (0.90)
  Pallas kernels: 51.4 us -> 46 us
    pallas_call x1, Pallas kernels: 51.4 us -> 46 us  [body(): pl.pallas_call(kernel, out_shape=(shape, shape), in_specs=[hbm, hbm, hbm]...]
where the time goes in v3:
time: 48.8 us; the launch traced here: 48.6 us
  Pallas kernels  46 us (94%)
  local copies, waits for them, and re-layouts  1.96 us (4%)
  between operations  0.65 us (1%)
    pallas_call x1, Pallas kernels, body(): pl.pallas_call(kernel, out_shape=(shape, shape), in_specs=[hbm, hbm, hbm]...  46 us
    unnamed x4, local copies, waits for them, and re-layouts  1.96 us

profile of v3, /device:TPU:1, one launch (start us, length us, event | category | flops | bytes accessed | tf_op | source)
XLA Modules:
  0.0 48.6 jit_solution(17460563091025898972)
XLA Ops:
  0.6 46.0 %shard_map.50 = (f32[3,2,2,4,128]{4,3,2,1,0:T(4,128)}, f32[3,2,2,4,128]{4,3,2,1,0:T(4,128)}) custom-call(f32[3,2,2,4,128]{4,3,2,1,0:T(4,128)} %pos_hbm.1, f32[3,2,2,4,128]{4,3,2,1,0:T(4,128)} %vel_hbm.1, s32[2,2,4]{2,1,0:T(2,128)} %cnt_hbm.1), custom_call_target="tpu_custom_call" | custom-call | tf_op jit(solution)/shard_map/pallas_call | solution.py:391
  46.7 0.0 copy-start
  46.7 1.4 %copy.7 = f32[3,2,2,4,128]{4,3,2,1,0:T(4,128)} copy(f32[3,2,2,4,128]{4,3,2,1,0:T(4,128)} %get-tuple-element.4) | data formatting | bytes 49152
  48.0 0.0 copy-done
  48.0 0.6 %copy.8 = f32[3,2,2,4,128]{4,3,2,1,0:T(4,128)} copy(f32[3,2,2,4,128]{4,3,2,1,0:T(4,128)S(1)} %copy-done) | data formatting | bytes 49152
Async XLA Ops:
  46.7 1.4 %copy-start = (f32[3,2,2,4,128]{4,3,2,1,0:T(4,128)S(1)}, f32[3,2,2,4,128]{4,3,2,1,0:T(4,128)}, u32[]{:S(2)}) copy-start(f32[3,2,2,4,128]{4,3,2,1,0:T(4,128)} %get-tuple-element.5) | copy-start | bytes 73732

commit v4 on v3

--- a/solution.py
+++ b/solution.py
@@ -57,7 +57,7 @@
 
 def kernel(
     pos_hbm, vel_hbm, cnt_hbm, vout_ref, mout_ref,
-    pos_ref, vel_ref, cnt_ref, ext, gext, lhs, mom, wts, pwts, gwide, grow, own_part_a, wide_p, wide_r, single_p, single_r, dens, push,
+    pos_ref, vel_ref, cnt_ref, ext, gext, lhs, mom, wts, pwts, gwide, grow, spread, own_p, own_r, wide_p, wide_r, single_p, single_r, dens, push,
     load_sem, send_sem, recv_sem, gsend_sem, grecv_sem,
 ):
     loads = [
@@ -137,11 +137,9 @@
         high, low, rest = split3(jnp.where(row4 == 3, norm, point))
         ones = jnp.ones_like(high)
         stack = jnp.concatenate([high, high, high, low, low, rest, ones, jnp.zeros_like(ones)], axis=0)
-        j = (x * 4 + y, z)
-        lhs[j] = stack.T.astype(BF16)
         moments = jnp.concatenate([high, low, rest, ones], axis=0).astype(BF16)
-        mom[j] = jnp.concatenate([moments, moments], axis=1)
-        return point, norm
+        mom[x * 4 + y, z] = jnp.concatenate([moments, moments], axis=1)
+        return point, norm, stack.T.astype(BF16)
 
     def pair_columns(k):
         side = lax.rem(k, 2)
@@ -153,7 +151,8 @@
     def own_step(q, carry):
         x, y = own_column(q)
         for z in range(4):
-            point, norm = expand(x, y, z + 1)
+            point, norm, left = expand(x, y, z + 1)
+            lhs[q, z + 1] = left
             blocks = []
             for unit in (LOG2E, 1.0):
                 high, low, rest = split3(jnp.where(row4 == 3, unit, (0.5 * unit) * point))
@@ -184,8 +183,8 @@
     edge_pairs = [(0, 0), (3, 5)]
     all_pairs = [(iz, iz + dz) for iz in range(4) for dz in range(3)]
 
-    def density_tile(j, weight, masked, stores, slot):
-        both = jnp.dot(lhs[j], weight, preferred_element_type=F32)
+    def density_tile(left, weight, masked, stores, slot):
+        both = jnp.dot(left, weight, preferred_element_type=F32)
         width = both.shape[1] // 2
         fall = jnp.exp2(both[:, 0:width])
         remain = jnp.maximum(both[:, width:], 0.0)
@@ -195,41 +194,60 @@
             remain = jnp.concatenate(halves, axis=1)
         part = remain * fall
         rho = part * remain
-        if len(stores) == 1:
-            stores[0][slot] = part
-        else:
-            mixed = rho + part
-            stores[0][slot] = mixed * fall
-            stores[1][slot] = mixed + part
+        mixed = rho + part
+        stores[0][slot] = mixed * fall
+        stores[1][slot] = mixed + part
         return jnp.sum(rho.reshape(16, 8, width), axis=0)
 
-    def force_tile(j, weight, grad, stores, slot):
-        width = grad.shape[1]
-        column, z = j
-        other = gwide[column, :, z * 128 : z * 128 + 128]
-        if width == 256:
+    def force_tile(j, other, grad, stores, slot):
+        if grad.shape[1] == 256:
             other = jnp.concatenate([other, other], axis=1)
-        sums = other + grad
-        if len(stores) == 1:
-            both = jnp.dot(lhs[j], weight, preferred_element_type=F32)
-            fall = jnp.exp2(both[:, 0:width])
-            factor = stores[0][slot] * ((both[:, width:] + 1.0) * (fall + sums) + sums)
-        else:
-            factor = stores[0][slot] + stores[1][slot] * sums
+        factor = stores[0][slot] + stores[1][slot] * (other + grad)
         high = factor.astype(BF16)
         low = (factor - high.astype(F32)).astype(BF16)
         return jnp.dot(mom[j], jnp.concatenate([high, low], axis=0), preferred_element_type=F32)
 
-    def group(kind, bases, weights, items, stores, slot, first=False):
+    row8 = lax.broadcasted_iota(jnp.int32, (8, 128), 0)
+
+    def grad_column(x, y, inside):
+        rows = []
+        for z in range(6):
+            if z not in inside:
+                rows.append(jnp.zeros((8, 128), F32))
+                continue
+            high, low, rest = split3(GRAD_SCALE * gext[x, y, z])
+            rows.append(
+                jnp.where(row8 == 0, high, jnp.where(row8 == 1, low, jnp.where(row8 == 2, rest, 0.0)))
+            )
+        turned = jnp.concatenate(rows, axis=0).T.astype(BF16)
+        return jnp.dot(turned, spread[...], preferred_element_type=F32)
+
+    def own_index(column):
+        if isinstance(column, int):
+            return (column // 4 - 1) * 2 + column % 4 - 1
+        return (column // 4 - 1) * 2 + lax.rem(column, 4) - 1
+
+    def own_cells(kind, column):
+        if kind == "density":
+            return lambda z: lhs[own_index(column), z]
+        return lambda z: gwide[own_index(column), :, z * 128 : z * 128 + 128]
+
+    def halo_cells(kind, column):
+        x, y = column // 4, lax.rem(column, 4)
+        if kind == "density":
+            lefts = [expand(x, y, z)[2] for z in range(6)]
+            return lambda z: lefts[z]
+        wide_grad = grad_column(x, y, range(6))
+        return lambda z: wide_grad[:, z * 128 : z * 128 + 128]
+
+    def group(kind, bases, weights, cells, items, stores, slot, first=False):
         totals = {}
         for n, (column, iz, jz, masked) in enumerate(items):
-            j = (column, jz)
-            weight = weights(iz)
             if kind == "density":
-                part = density_tile(j, weight, masked, stores, slot + n)
+                part = density_tile(cells(column)(jz), weights(iz), masked, stores, slot + n)
             else:
                 grad = jnp.concatenate([grow[base + iz] for base in bases], axis=1)
-                part = force_tile(j, weight, grad, stores, slot + n)
+                part = force_tile((column, jz), cells(column)(jz), grad, stores, slot + n)
             totals[iz] = part if iz not in totals else totals[iz] + part
         target = dens if kind == "density" else push
         for iz, total in totals.items():
@@ -237,9 +255,9 @@
                 block = total[:, h * 128 : h * 128 + 128]
                 target[base + iz] = block if first else target[base + iz] + block
 
-    def pair_group(kind, k, items, stores, slot, first=False):
+    def pair_group(kind, k, cells, items, stores, slot, first=False):
         one, two = pair_columns(k)
-        group(kind, [one * 4, two * 4], lambda iz: pwts[k * 4 + iz], items, stores, slot, first)
+        group(kind, [one * 4, two * 4], lambda iz: pwts[k * 4 + iz], cells, items, stores, slot, first)
 
     def own_part(kind):
         def same_step(k, carry):
@@ -249,13 +267,14 @@
                 for h, column in enumerate(columns)
                 for iz, jz in own_pairs
             ]
-            pair_group(kind, k, items, [own_part_a], k * 20, True)
+            pair_group(kind, k, lambda c: own_cells(kind, c), items, [own_p, own_r], k * 20, True)
             return carry
 
         def other_step(p, carry):
             k = p // 2
             column = (2 - k) * 4 + 1 + lax.rem(p, 2)
-            pair_group(kind, k, [(column, iz, jz, None) for iz, jz in own_pairs], [own_part_a], 40 + p * 10)
+            items = [(column, iz, jz, None) for iz, jz in own_pairs]
+            pair_group(kind, k, lambda c: own_cells(kind, c), items, [own_p, own_r], 40 + p * 10)
             return carry
 
         lax.fori_loop(0, 2, same_step, 0)
@@ -264,7 +283,7 @@
     def halo_part(kind):
         def edge_step(k, carry):
             items = [(c, iz, jz, None) for c in (5, 6, 9, 10) for iz, jz in edge_pairs]
-            pair_group(kind, k, items, [wide_p, wide_r], k * 8)
+            pair_group(kind, k, lambda c: own_cells(kind, c), items, [wide_p, wide_r], k * 8)
             return carry
 
         def face_step(p, carry):
@@ -272,13 +291,16 @@
             side = 1 + lax.rem(k, 2)
             near = k < 2
             column = jnp.where(near, 4 * (3 * (side - 1)) + 1 + far, 4 * (1 + far) + 3 * (side - 1))
-            pair_group(kind, k, [(column, iz, jz, None) for iz, jz in all_pairs], [wide_p, wide_r], 16 + p * 12)
+            items = [(column, iz, jz, None) for iz, jz in all_pairs]
+            cells = halo_cells(kind, column)
+            pair_group(kind, k, lambda c: cells, items, [wide_p, wide_r], 16 + p * 12)
             return carry
 
         def corner_step(q, carry):
             column = 12 * (q // 2) + 3 * lax.rem(q, 2)
+            cells = halo_cells(kind, column)
             group(
-                kind, [q * 4], lambda iz: wts[q * 4 + iz],
+                kind, [q * 4], lambda iz: wts[q * 4 + iz], lambda c: cells,
                 [(column, iz, jz, None) for iz, jz in all_pairs], [single_p, single_r], q * 12,
             )
             return carry
@@ -287,32 +309,18 @@
         lax.fori_loop(0, 8, face_step, 0)
         lax.fori_loop(0, 4, corner_step, 0)
 
-    def halo_column(k):
-        x = jnp.where(k < 4, 0, jnp.where(k < 8, 3, 1 + lax.rem(k, 2)))
-        y = jnp.where(k < 8, lax.rem(k, 4), jnp.where(k < 10, 0, 3))
-        return x, y
-
     own_part("density")
 
     for copy in copies:
         copy.wait()
 
-    def halo_expand(k, carry):
-        for n in range(2):
-            x, y = halo_column(2 * k + n)
-            for z in range(6):
-                expand(x, y, z)
+    def edge_expand(x, carry):
+        for y in (1, 2):
+            for z in (0, 5):
+                lhs[2 * x + y - 1, z] = expand(x + 1, y, z)[2]
         return carry
 
-    def edge_expand(q, carry):
-        x = q + 1
-        for y in (1, 2):
-            expand(x, y, 0)
-            expand(x, y, 5)
-        return carry
-
     lax.fori_loop(0, 2, edge_expand, 0)
-    lax.fori_loop(0, 6, halo_expand, 0)
 
     halo_part("density")
 
@@ -326,41 +334,24 @@
     lax.fori_loop(0, 4, grad_step, 0)
     copies = exchange(gext, gsend_sem, grecv_sem)
 
-    row8 = lax.broadcasted_iota(jnp.int32, (8, 128), 0)
-
-    def grad_column(x, y, inner):
-        rows = []
-        for z in range(6):
-            if inner and z in (0, 5):
-                rows.append(jnp.zeros((8, 128), F32))
-                continue
-            high, low, rest = split3(GRAD_SCALE * gext[x, y, z])
-            rows.append(
-                jnp.where(row8 == 0, high, jnp.where(row8 == 1, low, jnp.where(row8 == 2, rest, 0.0)))
-            )
-        turned = jnp.concatenate(rows, axis=0).T.astype(BF16)
-        gwide[x * 4 + y] = jnp.dot(turned, spread, preferred_element_type=F32)
-
     spread_row = lax.broadcasted_iota(jnp.int32, (GRAD_ROWS, 768), 0) // 8
     spread_lane = lax.broadcasted_iota(jnp.int32, (GRAD_ROWS, 768), 1) // 128
-    spread = jnp.where(spread_row == spread_lane, 1.0, 0.0).astype(BF16)
+    spread[...] = jnp.where(spread_row == spread_lane, 1.0, 0.0).astype(BF16)
 
     for q in range(4):
         for z in range(4):
             grow[q * 4 + z] = GRAD_SCALE * gext[1 + q // 2, 1 + q % 2, z + 1]
-        grad_column(1 + q // 2, 1 + q % 2, True)
+        gwide[q] = grad_column(1 + q // 2, 1 + q % 2, range(1, 5))
 
     own_part("force")
 
     for copy in copies:
         copy.wait()
 
-    def row_grad(x, carry):
-        for y in range(4):
-            grad_column(x, y, False)
-        return carry
-
-    lax.fori_loop(0, 4, row_grad, 0)
+    for q in range(4):
+        edges = grad_column(1 + q // 2, 1 + q % 2, (0, 5))
+        gwide[q, :, 0:128] = edges[:, 0:128]
+        gwide[q, :, 640:768] = edges[:, 640:768]
 
     halo_part("force")
 
@@ -399,12 +390,14 @@
             pltpu.SMEM(counts.shape, jnp.int32),
             pltpu.VMEM(EXT + (4, 128), F32),
             pltpu.VMEM(EXT + (1, 128), F32),
-            pltpu.VMEM((COLUMNS, 6, 128, 32), BF16),
+            pltpu.VMEM((4, 6, 128, 32), BF16),
             pltpu.VMEM((COLUMNS, 6, 16, 256), BF16),
             pltpu.VMEM((CELLS, 32, 256), BF16),
             pltpu.VMEM((CELLS, 32, 512), BF16),
-            pltpu.VMEM((COLUMNS, 128, 768), F32),
+            pltpu.VMEM((4, 128, 768), F32),
             pltpu.VMEM((CELLS, 1, 128), F32),
+            pltpu.VMEM((GRAD_ROWS, 768), BF16),
+            pltpu.VMEM((80, 128, 256), F32),
             pltpu.VMEM((80, 128, 256), F32),
             pltpu.VMEM((112, 128, 256), F32),
             pltpu.VMEM((112, 128, 256), F32),
@@ -419,7 +412,7 @@
             pltpu.SemaphoreType.DMA((links,)),
         ],
         compiler_params=pltpu.CompilerParams(
-            collective_id=0, has_side_effects=True, vmem_limit_bytes=60 * 1024 * 1024
+            collective_id=0, has_side_effects=True, vmem_limit_bytes=62 * 1024 * 1024
         ),
     )(positions, velocities, counts)
 

time: 48.8 us -> 42.7 us (0.88)
  Pallas kernels: 46 us -> 39.8 us
    pallas_call x1, Pallas kernels: 46 us -> 39.8 us  [body(): pl.pallas_call(kernel, out_shape=(shape, shape), in_specs=[hbm, hbm, hbm]...]
where the time goes in v4:
time: 42.7 us; the launch traced here: 42.4 us
  Pallas kernels  39.8 us (93%)
  local copies, waits for them, and re-layouts  1.96 us (5%)
  between operations  0.65 us (2%)
    pallas_call x1, Pallas kernels, body(): pl.pallas_call(kernel, out_shape=(shape, shape), in_specs=[hbm, hbm, hbm]...  39.8 us
    unnamed x4, local copies, waits for them, and re-layouts  1.96 us

profile of v4, /device:TPU:1, one launch (start us, length us, event | category | flops | bytes accessed | tf_op | source)
XLA Modules:
  0.0 42.4 jit_solution(14804977182031272009)
XLA Ops:
  0.6 39.8 %shard_map.50 = (f32[3,2,2,4,128]{4,3,2,1,0:T(4,128)}, f32[3,2,2,4,128]{4,3,2,1,0:T(4,128)}) custom-call(f32[3,2,2,4,128]{4,3,2,1,0:T(4,128)} %pos_hbm.1, f32[3,2,2,4,128]{4,3,2,1,0:T(4,128)} %vel_hbm.1, s32[2,2,4]{2,1,0:T(2,128)} %cnt_hbm.1), custom_call_target="tpu_custom_call" | custom-call | tf_op jit(solution)/shard_map/pallas_call | solution.py:382
  40.5 0.0 copy-start
  40.5 1.4 %copy.7 = f32[3,2,2,4,128]{4,3,2,1,0:T(4,128)} copy(f32[3,2,2,4,128]{4,3,2,1,0:T(4,128)} %get-tuple-element.4) | data formatting | bytes 49152
  41.8 0.0 copy-done
  41.8 0.6 %copy.8 = f32[3,2,2,4,128]{4,3,2,1,0:T(4,128)} copy(f32[3,2,2,4,128]{4,3,2,1,0:T(4,128)S(1)} %copy-done) | data formatting | bytes 49152
Async XLA Ops:
  40.5 1.4 %copy-start = (f32[3,2,2,4,128]{4,3,2,1,0:T(4,128)S(1)}, f32[3,2,2,4,128]{4,3,2,1,0:T(4,128)}, u32[]{:S(2)}) copy-start(f32[3,2,2,4,128]{4,3,2,1,0:T(4,128)} %get-tuple-element.5) | copy-start | bytes 73732

commit v5 on v4

--- a/solution.py
+++ b/solution.py
@@ -242,12 +242,12 @@
 
     def group(kind, bases, weights, cells, items, stores, slot, first=False):
         totals = {}
-        for n, (column, iz, jz, masked) in enumerate(items):
+        for n, (column, iz, jz, masked, *place) in enumerate(items):
             if kind == "density":
                 part = density_tile(cells(column)(jz), weights(iz), masked, stores, slot + n)
             else:
                 grad = jnp.concatenate([grow[base + iz] for base in bases], axis=1)
-                part = force_tile((column, jz), cells(column)(jz), grad, stores, slot + n)
+                part = force_tile(((place or [column])[0], jz), cells(column)(jz), grad, stores, slot + n)
             totals[iz] = part if iz not in totals else totals[iz] + part
         target = dens if kind == "density" else push
         for iz, total in totals.items():
@@ -286,28 +286,33 @@
             pair_group(kind, k, lambda c: own_cells(kind, c), items, [wide_p, wide_r], k * 8)
             return carry
 
-        def face_step(p, carry):
-            k, far = p // 2, lax.rem(p, 2)
+        def face_step(k, carry):
             side = 1 + lax.rem(k, 2)
             near = k < 2
-            column = jnp.where(near, 4 * (3 * (side - 1)) + 1 + far, 4 * (1 + far) + 3 * (side - 1))
-            items = [(column, iz, jz, None) for iz, jz in all_pairs]
-            cells = halo_cells(kind, column)
-            pair_group(kind, k, lambda c: cells, items, [wide_p, wide_r], 16 + p * 12)
+            cells, items = {}, []
+            for far in range(2):
+                column = jnp.where(
+                    near, 4 * (3 * (side - 1)) + 1 + far, 4 * (1 + far) + 3 * (side - 1)
+                )
+                cells[far] = halo_cells(kind, column)
+                items += [(far, iz, jz, None, column) for iz, jz in all_pairs]
+            pair_group(kind, k, lambda c: cells[c], items, [wide_p, wide_r], 16 + k * 24)
             return carry
 
-        def corner_step(q, carry):
-            column = 12 * (q // 2) + 3 * lax.rem(q, 2)
-            cells = halo_cells(kind, column)
-            group(
-                kind, [q * 4], lambda iz: wts[q * 4 + iz], lambda c: cells,
-                [(column, iz, jz, None) for iz, jz in all_pairs], [single_p, single_r], q * 12,
-            )
+        def corner_step(q_x, carry):
+            for q_y in range(2):
+                q = q_x * 2 + q_y
+                column = 12 * q_x + 3 * q_y
+                cells = halo_cells(kind, column)
+                group(
+                    kind, [q * 4], lambda iz: wts[q * 4 + iz], lambda c: cells,
+                    [(column, iz, jz, None) for iz, jz in all_pairs], [single_p, single_r], q * 12,
+                )
             return carry
 
         lax.fori_loop(0, 2, edge_step, 0)
-        lax.fori_loop(0, 8, face_step, 0)
-        lax.fori_loop(0, 4, corner_step, 0)
+        lax.fori_loop(0, 4, face_step, 0)
+        lax.fori_loop(0, 2, corner_step, 0)
 
     own_part("density")
 

time: 42.7 us -> 39.6 us (0.927)
  Pallas kernels: 39.8 us -> 36.8 us
    pallas_call x1, Pallas kernels: 39.8 us -> 36.8 us  [body(): pl.pallas_call(kernel, out_shape=(shape, shape), in_specs=[hbm, hbm, hbm]...]
where the time goes in v5:
time: 39.6 us; the launch traced here: 39.4 us
  Pallas kernels  36.8 us (93%)
  local copies, waits for them, and re-layouts  1.96 us (5%)
  between operations  0.65 us (2%)
    pallas_call x1, Pallas kernels, body(): pl.pallas_call(kernel, out_shape=(shape, shape), in_specs=[hbm, hbm, hbm]...  36.8 us
    unnamed x4, local copies, waits for them, and re-layouts  1.96 us

profile of v5, /device:TPU:1, one launch (start us, length us, event | category | flops | bytes accessed | tf_op | source)
XLA Modules:
  0.0 39.4 jit_solution(16777032857407852468)
XLA Ops:
  0.6 36.8 %shard_map.50 = (f32[3,2,2,4,128]{4,3,2,1,0:T(4,128)}, f32[3,2,2,4,128]{4,3,2,1,0:T(4,128)}) custom-call(f32[3,2,2,4,128]{4,3,2,1,0:T(4,128)} %pos_hbm.1, f32[3,2,2,4,128]{4,3,2,1,0:T(4,128)} %vel_hbm.1, s32[2,2,4]{2,1,0:T(2,128)} %cnt_hbm.1), custom_call_target="tpu_custom_call" | custom-call | tf_op jit(solution)/shard_map/pallas_call | solution.py:387
  37.4 0.0 copy-start
  37.5 1.4 %copy.7 = f32[3,2,2,4,128]{4,3,2,1,0:T(4,128)} copy(f32[3,2,2,4,128]{4,3,2,1,0:T(4,128)} %get-tuple-element.4) | data formatting | bytes 49152
  38.8 0.0 copy-done
  38.8 0.6 %copy.8 = f32[3,2,2,4,128]{4,3,2,1,0:T(4,128)} copy(f32[3,2,2,4,128]{4,3,2,1,0:T(4,128)S(1)} %copy-done) | data formatting | bytes 49152
Async XLA Ops:
  37.4 1.4 %copy-start = (f32[3,2,2,4,128]{4,3,2,1,0:T(4,128)S(1)}, f32[3,2,2,4,128]{4,3,2,1,0:T(4,128)}, u32[]{:S(2)}) copy-start(f32[3,2,2,4,128]{4,3,2,1,0:T(4,128)} %get-tuple-element.5) | copy-start | bytes 73732

commit v6 on v5

--- a/solution.py
+++ b/solution.py
@@ -296,47 +296,35 @@
                 )
                 cells[far] = halo_cells(kind, column)
                 items += [(far, iz, jz, None, column) for iz, jz in all_pairs]
+            corner = 12 * (k // 2) + 3 * side - 3
+            corner_cells = halo_cells(kind, corner)
             pair_group(kind, k, lambda c: cells[c], items, [wide_p, wide_r], 16 + k * 24)
-            return carry
-
-        def corner_step(q_x, carry):
-            for q_y in range(2):
-                q = q_x * 2 + q_y
-                column = 12 * q_x + 3 * q_y
-                cells = halo_cells(kind, column)
-                group(
-                    kind, [q * 4], lambda iz: wts[q * 4 + iz], lambda c: cells,
-                    [(column, iz, jz, None) for iz, jz in all_pairs], [single_p, single_r], q * 12,
-                )
+            group(
+                kind, [k * 4], lambda iz: wts[k * 4 + iz], lambda c: corner_cells,
+                [(corner, iz, jz, None) for iz, jz in all_pairs], [single_p, single_r], k * 12,
+            )
             return carry
 
         lax.fori_loop(0, 2, edge_step, 0)
         lax.fori_loop(0, 4, face_step, 0)
-        lax.fori_loop(0, 2, corner_step, 0)
 
     own_part("density")
 
     for copy in copies:
         copy.wait()
 
-    def edge_expand(x, carry):
-        for y in (1, 2):
-            for z in (0, 5):
-                lhs[2 * x + y - 1, z] = expand(x + 1, y, z)[2]
-        return carry
-
-    lax.fori_loop(0, 2, edge_expand, 0)
+    for q in range(4):
+        for z in (0, 5):
+            lhs[q, z] = expand(1 + q // 2, 1 + q % 2, z)[2]
 
     halo_part("density")
 
-    def grad_step(q, carry):
-        x, y = own_column(q)
+    for q in range(4):
+        x, y = 1 + q // 2, 1 + q % 2
         for z in range(4):
             density = RHO_SCALE * jnp.sum(dens[q * 4 + z], axis=0, keepdims=True)
             gext[x, y, z + 1] = ext[x, y, z + 1, 3:4, :] * 2.0 * (density - 1.0)
-        return carry
-
-    lax.fori_loop(0, 4, grad_step, 0)
+
     copies = exchange(gext, gsend_sem, grecv_sem)
 
     spread_row = lax.broadcasted_iota(jnp.int32, (GRAD_ROWS, 768), 0) // 8
@@ -360,8 +348,8 @@
 
     halo_part("force")
 
-    def finish(q, carry):
-        x, y = own_column(q)
+    for q in range(4):
+        x, y = 1 + q // 2, 1 + q % 2
         for z in range(4):
             total = push[q * 4 + z]
             point = shifted(x, y, z + 1)
@@ -374,9 +362,6 @@
                 mout_ref[c, x - 1, y - 1, z : z + 1, :] = (
                     (place + TIME_STEP * velocity) - place
                 ) * live
-        return carry
-
-    lax.fori_loop(0, 4, finish, 0)
 
 
 def body(positions, velocities, counts):

time: 39.6 us -> 38.5 us (0.972)
  Pallas kernels: 36.8 us -> 35.7 us
    pallas_call x1, Pallas kernels: 36.8 us -> 35.7 us  [body(): pl.pallas_call(kernel, out_shape=(shape, shape), in_specs=[hbm, hbm, hbm]...]
where the time goes in v6:
time: 38.5 us; the launch traced here: 38.3 us
  Pallas kernels  35.7 us (93%)
  local copies, waits for them, and re-layouts  1.96 us (5%)
  between operations  0.65 us (2%)
    pallas_call x1, Pallas kernels, body(): pl.pallas_call(kernel, out_shape=(shape, shape), in_specs=[hbm, hbm, hbm]...  35.7 us
    unnamed x4, local copies, waits for them, and re-layouts  1.96 us

profile of v6, /device:TPU:1, one launch (start us, length us, event | category | flops | bytes accessed | tf_op | source)
XLA Modules:
  0.0 38.3 jit_solution(12920145798144334813)
XLA Ops:
  0.6 35.7 %shard_map.50 = (f32[3,2,2,4,128]{4,3,2,1,0:T(4,128)}, f32[3,2,2,4,128]{4,3,2,1,0:T(4,128)}) custom-call(f32[3,2,2,4,128]{4,3,2,1,0:T(4,128)} %pos_hbm.1, f32[3,2,2,4,128]{4,3,2,1,0:T(4,128)} %vel_hbm.1, s32[2,2,4]{2,1,0:T(2,128)} %cnt_hbm.1), custom_call_target="tpu_custom_call" | custom-call | tf_op jit(solution)/shard_map/pallas_call | solution.py:372
  36.3 0.0 copy-start
  36.3 1.4 %copy.7 = f32[3,2,2,4,128]{4,3,2,1,0:T(4,128)} copy(f32[3,2,2,4,128]{4,3,2,1,0:T(4,128)} %get-tuple-element.4) | data formatting | bytes 49152
  37.7 0.0 copy-done
  37.7 0.6 %copy.8 = f32[3,2,2,4,128]{4,3,2,1,0:T(4,128)} copy(f32[3,2,2,4,128]{4,3,2,1,0:T(4,128)S(1)} %copy-done) | data formatting | bytes 49152
Async XLA Ops:
  36.3 1.4 %copy-start = (f32[3,2,2,4,128]{4,3,2,1,0:T(4,128)S(1)}, f32[3,2,2,4,128]{4,3,2,1,0:T(4,128)}, u32[]{:S(2)}) copy-start(f32[3,2,2,4,128]{4,3,2,1,0:T(4,128)} %get-tuple-element.5) | copy-start | bytes 73732

commit v7 on v6

--- a/solution.py
+++ b/solution.py
@@ -281,11 +281,6 @@
         lax.fori_loop(0, 4, other_step, 0)
 
     def halo_part(kind):
-        def edge_step(k, carry):
-            items = [(c, iz, jz, None) for c in (5, 6, 9, 10) for iz, jz in edge_pairs]
-            pair_group(kind, k, lambda c: own_cells(kind, c), items, [wide_p, wide_r], k * 8)
-            return carry
-
         def face_step(k, carry):
             side = 1 + lax.rem(k, 2)
             near = k < 2
@@ -296,6 +291,11 @@
                 )
                 cells[far] = halo_cells(kind, column)
                 items += [(far, iz, jz, None, column) for iz, jz in all_pairs]
+            edge, half = k // 2, lax.rem(k, 2)
+            edges = [(4 * (1 + half) + c, iz, jz, None) for c in (1, 2) for iz, jz in edge_pairs]
+            pair_group(
+                kind, edge, lambda c: own_cells(kind, c), edges, [wide_p, wide_r], edge * 8 + half * 4
+            )
             corner = 12 * (k // 2) + 3 * side - 3
             corner_cells = halo_cells(kind, corner)
             pair_group(kind, k, lambda c: cells[c], items, [wide_p, wide_r], 16 + k * 24)
@@ -305,7 +305,6 @@
             )
             return carry
 
-        lax.fori_loop(0, 2, edge_step, 0)
         lax.fori_loop(0, 4, face_step, 0)
 
     own_part("density")

time: 38.5 us -> 37.6 us (0.977)
  Pallas kernels: 35.7 us -> 34.7 us
    pallas_call x1, Pallas kernels: 35.7 us -> 34.7 us  [body(): pl.pallas_call(kernel, out_shape=(shape, shape), in_specs=[hbm, hbm, hbm]...]
where the time goes in v7:
time: 37.6 us; the launch traced here: 37.3 us
  Pallas kernels  34.7 us (92%)
  local copies, waits for them, and re-layouts  1.96 us (5%)
  between operations  0.65 us (2%)
    pallas_call x1, Pallas kernels, body(): pl.pallas_call(kernel, out_shape=(shape, shape), in_specs=[hbm, hbm, hbm]...  34.7 us
    unnamed x4, local copies, waits for them, and re-layouts  1.96 us

profile of v7, /device:TPU:1, one launch (start us, length us, event | category | flops | bytes accessed | tf_op | source)
XLA Modules:
  0.0 37.3 jit_solution(7872096816639438353)
XLA Ops:
  0.6 34.7 %shard_map.50 = (f32[3,2,2,4,128]{4,3,2,1,0:T(4,128)}, f32[3,2,2,4,128]{4,3,2,1,0:T(4,128)}) custom-call(f32[3,2,2,4,128]{4,3,2,1,0:T(4,128)} %pos_hbm.1, f32[3,2,2,4,128]{4,3,2,1,0:T(4,128)} %vel_hbm.1, s32[2,2,4]{2,1,0:T(2,128)} %cnt_hbm.1), custom_call_target="tpu_custom_call" | custom-call | tf_op jit(solution)/shard_map/pallas_call | solution.py:371
  35.4 0.0 copy-start
  35.4 1.4 %copy.7 = f32[3,2,2,4,128]{4,3,2,1,0:T(4,128)} copy(f32[3,2,2,4,128]{4,3,2,1,0:T(4,128)} %get-tuple-element.4) | data formatting | bytes 49152
  36.7 0.0 copy-done
  36.7 0.6 %copy.8 = f32[3,2,2,4,128]{4,3,2,1,0:T(4,128)} copy(f32[3,2,2,4,128]{4,3,2,1,0:T(4,128)S(1)} %copy-done) | data formatting | bytes 49152
Async XLA Ops:
  35.4 1.4 %copy-start = (f32[3,2,2,4,128]{4,3,2,1,0:T(4,128)S(1)}, f32[3,2,2,4,128]{4,3,2,1,0:T(4,128)}, u32[]{:S(2)}) copy-start(f32[3,2,2,4,128]{4,3,2,1,0:T(4,128)} %get-tuple-element.5) | copy-start | bytes 73732

commit v8 on v7

--- a/solution.py
+++ b/solution.py
@@ -209,7 +209,7 @@
 
     row8 = lax.broadcasted_iota(jnp.int32, (8, 128), 0)
 
-    def grad_column(x, y, inside):
+    def grad_turned(x, y, inside):
         rows = []
         for z in range(6):
             if z not in inside:
@@ -219,8 +219,10 @@
             rows.append(
                 jnp.where(row8 == 0, high, jnp.where(row8 == 1, low, jnp.where(row8 == 2, rest, 0.0)))
             )
-        turned = jnp.concatenate(rows, axis=0).T.astype(BF16)
-        return jnp.dot(turned, spread[...], preferred_element_type=F32)
+        return jnp.concatenate(rows, axis=0).T.astype(BF16)
+
+    def grad_column(x, y, inside):
+        return jnp.dot(grad_turned(x, y, inside), spread[...], preferred_element_type=F32)
 
     def own_index(column):
         if isinstance(column, int):
@@ -341,9 +343,9 @@
         copy.wait()
 
     for q in range(4):
-        edges = grad_column(1 + q // 2, 1 + q % 2, (0, 5))
-        gwide[q, :, 0:128] = edges[:, 0:128]
-        gwide[q, :, 640:768] = edges[:, 640:768]
+        turned = grad_turned(1 + q // 2, 1 + q % 2, (0, 5))
+        for lanes in (slice(0, 128), slice(640, 768)):
+            gwide[q, :, lanes] = jnp.dot(turned, spread[:, lanes], preferred_element_type=F32)
 
     halo_part("force")
 

time: 37.6 us -> 37.5 us (level)
  no operation moved by 1% of the time
where the time goes in v8:
time: 37.5 us; the launch traced here: 37.3 us
  Pallas kernels  34.7 us (93%)
  local copies, waits for them, and re-layouts  1.96 us (5%)
  between operations  0.65 us (2%)
    pallas_call x1, Pallas kernels, body(): pl.pallas_call(kernel, out_shape=(shape, shape), in_specs=[hbm, hbm, hbm]...  34.7 us
    unnamed x4, local copies, waits for them, and re-layouts  1.96 us

profile of v8, /device:TPU:1, one launch (start us, length us, event | category | flops | bytes accessed | tf_op | source)
XLA Modules:
  0.0 37.3 jit_solution(3155621948745798525)
XLA Ops:
  0.6 34.7 %shard_map.50 = (f32[3,2,2,4,128]{4,3,2,1,0:T(4,128)}, f32[3,2,2,4,128]{4,3,2,1,0:T(4,128)}) custom-call(f32[3,2,2,4,128]{4,3,2,1,0:T(4,128)} %pos_hbm.1, f32[3,2,2,4,128]{4,3,2,1,0:T(4,128)} %vel_hbm.1, s32[2,2,4]{2,1,0:T(2,128)} %cnt_hbm.1), custom_call_target="tpu_custom_call" | custom-call | tf_op jit(solution)/shard_map/pallas_call | solution.py:373
  35.3 0.0 copy-start
  35.3 1.4 %copy.7 = f32[3,2,2,4,128]{4,3,2,1,0:T(4,128)} copy(f32[3,2,2,4,128]{4,3,2,1,0:T(4,128)} %get-tuple-element.4) | data formatting | bytes 49152
  36.7 0.0 copy-done
  36.7 0.6 %copy.8 = f32[3,2,2,4,128]{4,3,2,1,0:T(4,128)} copy(f32[3,2,2,4,128]{4,3,2,1,0:T(4,128)S(1)} %copy-done) | data formatting | bytes 49152
Async XLA Ops:
  35.3 1.4 %copy-start = (f32[3,2,2,4,128]{4,3,2,1,0:T(4,128)S(1)}, f32[3,2,2,4,128]{4,3,2,1,0:T(4,128)}, u32[]{:S(2)}) copy-start(f32[3,2,2,4,128]{4,3,2,1,0:T(4,128)} %get-tuple-element.5) | copy-start | bytes 73732
